TPU v7x, 32 devices: a whole 2x2x4 slice. The times are simulated.
32 devices in a mesh: gx: 4 (over z), gy: 8 (over y, x, core).
Axes of the slice: x: 2, y: 2, z: 4, core: 2. Of those that a mesh axis runs over, the one named last changes fastest.
Arguments:
- pdf: float32 [19, 64, 1024], P(None, 'gx', 'gy'), as said below
- grains: float32 [26, 4, 2048], P(None, 'gx', 'gy'), as said below
- grain_moves: int32 [4, 2048], P('gx', 'gy'), may hold values from 0 to 8, as said below
- owner_map: int32 [8, 16], P('gx', 'gy'), may hold values from 0 to 3, as said below
- link_lists: int32 [3, 8, 4096], P(None, 'gx', 'gy'), may hold values from 0 to 511, as said below
Outputs:
- moved_blocks: float32 [16, 8, 19, 512], P('gx', 'gy')
- new_grains: float32 [26, 4, 2560], P(None, 'gx', 'gy')
Inputs may be any that keep to these rules, and one draw needn't show every extreme that they name: `pdf`: each entry lies between 0.4 and 1.6 times its direction's lattice weight. `grains`: A grain's position lies inside the cells of the group that it belongs to after the move. `grain_moves`: at most 8 grains of one group move to any one of its eight neighbouring groups; every group moves at least one grain each way, and some group receives exactly 8 grains from each of its eight neighbours. `owner_map`: owners are gx indices in the block's own row of gy. At most 1 block of one group go to one owner, and in every row of gy one owner receives exactly 1 block from every group of that row. `link_lists`: row 0: a cell number of the block; row 1: a direction 1 to 18; row 2: a grain slot below 320. No cell appears twice among one block's links.
All inputs are finite; a program needn't handle non-finite values.
Results may differ from a plain program's by a relative error of at most 0.0003.
Values sent between devices are 32-bit elements; how exact they have to be, the bound alone decides.
A program may use at most 64 MiB of HBM per device.

v0:
```python
import jax
import jax.numpy as jnp
import numpy as np
from jax import lax
from jax.sharding import PartitionSpec as P

Q = 19
E = 8
Z = 8
BXD = 2
BYD = 2
GCAP = 8
CAPP = 1
LB = 256
CB = 512


lattice_vel = np.array(
    [
        [0, 0, 0],
        [1, 0, 0],
        [-1, 0, 0],
        [0, 1, 0],
        [0, -1, 0],
        [0, 0, 1],
        [0, 0, -1],
        [1, 1, 0],
        [-1, -1, 0],
        [1, -1, 0],
        [-1, 1, 0],
        [1, 0, 1],
        [-1, 0, -1],
        [1, 0, -1],
        [-1, 0, 1],
        [0, 1, 1],
        [0, -1, -1],
        [0, 1, -1],
        [0, -1, 1],
    ],
    dtype=np.int32,
)
lattice_wts = np.array([1.0 / 3.0] + [1.0 / 18.0] * 6 + [1.0 / 36.0] * 12, dtype=np.float32)
opposite_dir = np.array(
    [0, 2, 1, 4, 3, 6, 5, 8, 7, 10, 9, 12, 11, 14, 13, 16, 15, 18, 17], dtype=np.int32
)
velocity_cols = lattice_vel.astype(np.float32)
moment_rows = np.stack(
    [
        np.ones(19, np.float32),
        velocity_cols[:, 0],
        velocity_cols[:, 1],
        velocity_cols[:, 2],
        velocity_cols[:, 0] * velocity_cols[:, 0],
        velocity_cols[:, 1] * velocity_cols[:, 1],
        velocity_cols[:, 2] * velocity_cols[:, 2],
        velocity_cols[:, 0] * velocity_cols[:, 1],
        velocity_cols[:, 0] * velocity_cols[:, 2],
        velocity_cols[:, 1] * velocity_cols[:, 2],
    ]
).astype(np.float32)
dirs_every = np.arange(19, dtype=np.int32)
viscosity_zero = 0.1
viscosity_limit = 0.01
relax_zero = 0.8
carreau_time = 20.0
carreau_power = 0.5


def shifted(block, axis, distance):
    devices = range(lax.axis_size(axis))
    route = [((i - distance) % len(devices), i) for i in devices]
    return lax.ppermute(block, axis, route)


def with_halo(block, sides, width):
    for axis, dim in sides:
        count = lax.axis_size(axis)
        forward = [(i, i + 1) for i in range(count - 1)]
        forward.append((count - 1, 0))
        backward = [(target, source) for source, target in forward]
        low = lax.ppermute(
            lax.slice_in_dim(block, block.shape[dim] - width, None, axis=dim), axis, forward
        )
        high = lax.ppermute(lax.slice_in_dim(block, 0, width, axis=dim), axis, backward)
        block = jnp.concatenate([low, block, high], axis=dim)
    return block


def collide(populations):
    moments = jnp.dot(jnp.asarray(moment_rows), populations, precision=lax.Precision.HIGHEST)
    density = moments[0]
    velocity = moments[1:4] / density
    projected = jnp.dot(jnp.asarray(velocity_cols), velocity, precision=lax.Precision.HIGHEST)
    speed_sq = jnp.sum(velocity * velocity, axis=0)
    equilibrium = (
        jnp.asarray(lattice_wts)[:, None]
        * density
        * (1.0 + 3.0 * projected + 4.5 * projected * projected - 1.5 * speed_sq)
    )
    density_third = density / 3.0
    stress_xx = moments[4] - density_third - density * velocity[0] * velocity[0]
    stress_yy = moments[5] - density_third - density * velocity[1] * velocity[1]
    stress_zz = moments[6] - density_third - density * velocity[2] * velocity[2]
    stress_xy = moments[7] - density * velocity[0] * velocity[1]
    stress_xz = moments[8] - density * velocity[0] * velocity[2]
    stress_yz = moments[9] - density * velocity[1] * velocity[2]
    contracted = (
        stress_xx * stress_xx
        + stress_yy * stress_yy
        + stress_zz * stress_zz
        + 2.0 * (stress_xy * stress_xy + stress_xz * stress_xz + stress_yz * stress_yz)
    )
    shear_rate = 1.5 / (density * relax_zero) * jnp.sqrt(2.0 * contracted)
    viscosity = viscosity_limit + (viscosity_zero - viscosity_limit) * (
        1.0 + (carreau_time * shear_rate) ** 2
    ) ** (0.5 * (carreau_power - 1.0))
    relax_time = 3.0 * viscosity + 0.5
    return populations - (populations - equilibrium) / relax_time


def pack_grains(own_grains, move_code, slot_cap):
    moving = move_code != 4
    region = jnp.where(move_code > 4, move_code - 1, move_code)
    matches = (move_code[None, :] == jnp.arange(9, dtype=jnp.int32)[:, None]).astype(jnp.int32)
    rank_of = jnp.sum(
        matches * (jnp.cumsum(matches, axis=1, dtype=jnp.int32) - 1), axis=0, dtype=jnp.int32
    )
    target = region * slot_cap + rank_of
    placing = jnp.logical_and(
        target[:, None] == jnp.arange(8 * slot_cap, dtype=jnp.int32)[None, :], moving[:, None]
    ).astype(jnp.float32)
    packed = jnp.dot(own_grains, placing, precision=lax.Precision.HIGHEST)
    kept_grains = own_grains * (move_code == 4).astype(jnp.float32)[None, :]
    return (kept_grains, packed)


def link_correction(cell_ids, direction_ids, picked, block_x, block_y):
    vel_table = jnp.asarray(velocity_cols)
    step_x = vel_table[:, 0][direction_ids]
    step_y = vel_table[:, 1][direction_ids]
    step_z = vel_table[:, 2][direction_ids]
    local_x = cell_ids // (E * Z)
    local_y = cell_ids // Z % E
    local_z = cell_ids % Z
    middle_x = (block_x * E + local_x).astype(jnp.float32) + 0.5 * step_x
    middle_y = (block_y * E + local_y).astype(jnp.float32) + 0.5 * step_y
    middle_z = local_z.astype(jnp.float32) + 0.5 * step_z
    rel_x = middle_x - picked[0]
    rel_y = middle_y - picked[1]
    rel_z = middle_z - picked[2]
    wall_x = picked[3] + picked[7] * rel_z - picked[8] * rel_y
    wall_y = picked[4] + picked[8] * rel_x - picked[6] * rel_z
    wall_z = picked[5] + picked[6] * rel_y - picked[7] * rel_x
    return (
        6.0
        * jnp.asarray(lattice_wts)[direction_ids]
        * (step_x * wall_x + step_y * wall_y + step_z * wall_z)
    )


def block_ranks(owners):
    count_blocks = owners.shape[-1]
    matching = owners[..., :, None] == owners[..., None, :]
    earlier = jnp.arange(count_blocks)[None, :] < jnp.arange(count_blocks)[:, None]
    return jnp.sum(jnp.logical_and(matching, earlier).astype(jnp.int32), axis=-1, dtype=jnp.int32)


def extend(populations, picks):
    plus_x, minus_x, plus_y, minus_y = picks
    count_dirs = populations.shape[0]
    width_x = populations.shape[1]
    ghosts_x = []
    for offset, chosen, first_cell in ((1, plus_x, width_x - 1), (-1, minus_x, 0)):
        rim_cells = lax.slice_in_dim(populations, first_cell, first_cell + 1, axis=1)[chosen]
        arrived = shifted(rim_cells, "gx", offset)
        ghosts_x.append(
            jnp.zeros((count_dirs, 1, populations.shape[2]), populations.dtype)
            .at[chosen]
            .set(arrived)
        )
    widened = jnp.concatenate([ghosts_x[0], populations, ghosts_x[1]], axis=1)
    length_y = widened.shape[2]
    ghosts_y = []
    for offset, chosen, first_cell in ((1, plus_y, length_y - Z), (-1, minus_y, 0)):
        rim_cells = lax.slice_in_dim(widened, first_cell, first_cell + Z, axis=2)[chosen]
        arrived = shifted(rim_cells, "gy", offset)
        ghosts_y.append(
            jnp.zeros((count_dirs, widened.shape[1], Z), widened.dtype).at[chosen].set(arrived)
        )
    return jnp.concatenate([ghosts_y[0], widened, ghosts_y[1]], axis=2)


def stream_flat(collided):
    tile_cells = collided.shape[1]
    row_width = (E + 2) * Z
    depth_index = jnp.arange(tile_cells, dtype=jnp.int32) % Z
    outputs = []
    for direction in range(19):
        step_x = int(lattice_vel[direction, 0])
        step_y = int(lattice_vel[direction, 1])
        step_z = int(lattice_vel[direction, 2])
        offset = step_x * row_width + step_y * Z + step_z
        layer_cells = jnp.roll(collided[direction], offset)
        if step_z == 1:
            layer_cells = jnp.where(
                depth_index == 0, jnp.roll(collided[direction], offset - Z), layer_cells
            )
        elif step_z == -1:
            layer_cells = jnp.where(
                depth_index == Z - 1, jnp.roll(collided[direction], offset + Z), layer_cells
            )
        outputs.append(layer_cells)
    return jnp.stack(outputs)


def interior_of(flat_tile):
    return flat_tile.reshape(Q, E + 2, E + 2, Z)[:, 1 : E + 1, 1 : E + 1, :].reshape(Q * CB)


def finish_tile(tile_cells, extra_rows):
    filled = extra_rows[2, 0]
    populations = jnp.where(filled > 0.5, tile_cells, jnp.asarray(lattice_wts)[:, None])
    collided = collide(populations)
    passed = interior_of(stream_flat(collided))
    interior = interior_of(collided)
    codes_int = extra_rows[1].astype(jnp.int32)
    target = jnp.asarray(opposite_dir)[codes_int // CB] * CB + codes_int % CB
    values = interior[codes_int] - extra_rows[0]
    return (passed.at[target].set(values) * filled).reshape(Q, CB)


def settle_tiles(parts):
    tile_part, extra_part = parts
    senders = tile_part.shape[0]
    item_count = tile_part.shape[1]
    finished = jax.vmap(finish_tile)(
        tile_part.reshape((senders * item_count,) + tile_part.shape[2:]),
        extra_part.reshape((senders * item_count,) + extra_part.shape[2:]),
    )
    return finished.reshape(senders, item_count, Q, CB)


def body(pdf, grains, grain_moves, owner_map, link_lists):
    group_size = lax.axis_size("gx")
    place_x = lax.axis_index("gx")
    place_y = lax.axis_index("gy")
    own_grains = grains[:, 0, :]
    move_codes = grain_moves[0]
    kept_grains, packed = pack_grains(own_grains, move_codes, GCAP)
    holder = packed[:, None, None, :]
    beside_all = with_halo(holder, (("gx", 1), ("gy", 2)), 1)
    regions = []
    for move_code in (0, 1, 2, 3, 5, 6, 7, 8):
        step_x = move_code // 3 - 1
        step_y = move_code % 3 - 1
        region = move_code if move_code < 4 else move_code - 1
        regions.append(
            beside_all[:, 1 - step_x, 1 - step_y, :][:, region * GCAP : (region + 1) * GCAP]
        )
    incoming = jnp.concatenate(regions, axis=1)
    grain_table = jnp.concatenate([kept_grains, incoming], axis=1)
    link_rows = link_lists.reshape(3, BXD * BYD, LB)
    local_number = jnp.arange(BXD * BYD, dtype=jnp.int32)[:, None]
    block_x = place_x * BXD + local_number // BYD
    block_y = place_y * BYD + local_number % BYD
    cell_ids, direction_ids, grain_ids = (link_rows[0], link_rows[1], link_rows[2])
    picked = grain_table[:, grain_ids]
    correction = link_correction(cell_ids, direction_ids, picked, block_x, block_y)
    source = direction_ids * CB + cell_ids
    owners = owner_map.reshape(-1)
    slot_index = owners * CAPP + block_ranks(owners)
    extended = extend(pdf, (dirs_every, dirs_every, dirs_every, dirs_every))
    tile_list = []
    for tile_x in range(BXD):
        for tile_y in range(BYD):
            tile_list.append(
                extended[
                    :, tile_x * E : tile_x * E + E + 2, tile_y * E * Z : (tile_y * E + E + 2) * Z
                ].reshape(Q, -1)
            )
    tile_stack = jnp.stack(tile_list)
    extras = jnp.stack([correction, source.astype(jnp.float32), jnp.ones_like(correction)], axis=1)
    send_tiles = (
        jnp.zeros((group_size * CAPP,) + tile_stack.shape[1:], jnp.float32)
        .at[slot_index]
        .set(tile_stack)
    )
    send_extras = (
        jnp.zeros((group_size * CAPP,) + extras.shape[1:], jnp.float32).at[slot_index].set(extras)
    )
    send_tiles = send_tiles.reshape((group_size, CAPP) + tile_stack.shape[1:])
    send_extras = send_extras.reshape((group_size, CAPP) + extras.shape[1:])
    moved_blocks = settle_tiles(
        (
            lax.all_to_all(send_tiles, "gx", split_axis=0, concat_axis=0, tiled=True),
            lax.all_to_all(send_extras, "gx", split_axis=0, concat_axis=0, tiled=True),
        )
    )
    return (moved_blocks, grain_table[:, None, :])


def solution(mesh):
    in_specs = (
        P(None, "gx", "gy"),
        P(None, "gx", "gy"),
        P("gx", "gy"),
        P("gx", "gy"),
        P(None, "gx", "gy"),
    )
    out_specs = (P("gx", "gy", None, None), P(None, "gx", "gy"))
    return jax.shard_map(body, mesh=mesh, in_specs=in_specs, out_specs=out_specs, check_vma=False)
```

profile of v0, /device:TPU:0, one launch (start us, length us, event | category | flops | bytes accessed | tf_op | source)
XLA Modules:
  0.0 120.8 jit_solution(7160228314255595584)
XLA Ops:
  0.6 0.7 fusion.16
  1.3 0.6 reduce-window.6
  2.1 0.8 select_reduce_fusion
  2.9 0.7 broadcast_compare_fusion.1
  3.6 0.7 fusion.86
  4.3 1.0 convolution_bitcast_fusion.1
  5.3 3.1 %collective-permute-start = (f32[26,1,1,64]{3,0,2,1:T(8,128)S(1)}, f32[26,1,1,64]{3,0,2,1:T(8,128)S(1)}, u32[]{:S(2)}, u32[]{:S(2)}) collective-permute-start(f32[26,1,1,64]{3,0,2,1:T(8,128)S(1)} %convolution_bitcast_fusion.1), channel_id=1, source_target_pairs={{0,8},{8,16},{16,24},{24,0},{1,9},{9,17},{17,25},{25,1},{2,10},{10... | collective-permute-start | bytes 19976 | tf_op jit(solution)/shard_map/ppermute | solution.py:81
  8.4 2.1 %collective-permute-start.1 = (f32[26,1,1,64]{3,0,2,1:T(8,128)S(1)}, f32[26,1,1,64]{3,0,2,1:T(8,128)S(1)}, u32[]{:S(2)}, u32[]{:S(2)}) collective-permute-start(f32[26,1,1,64]{3,0,2,1:T(8,128)S(1)} %convolution_bitcast_fusion.1), channel_id=1, source_target_pairs={{8,0},{16,8},{24,16},{0,24},{9,1},{17,9},{25,17},{1,25},{10,2},{18... | collective-permute-start | bytes 19976 | tf_op jit(solution)/shard_map/ppermute | solution.py:84
  10.5 0.7 fusion.97
  11.2 0.9 fusion.96
  13.4 3.9 %collective-permute-start.5 = (f32[19,1,128]{2,0,1:T(8,128)S(1)}, f32[19,1,128]{2,0,1:T(8,128)S(1)}, u32[]{:S(2)}, u32[]{:S(2)}) collective-permute-start(f32[19,1,128]{2,0,1:T(8,128)S(1)} %bitcast.548), channel_id=1, source_target_pairs={{8,0},{16,8},{24,16},{0,24},{9,1},{17,9},{25,17},{1,25},{10,2},{18... | collective-permute-start | bytes 29192 | tf_op jit(solution)/shard_map/ppermute | solution.py:72
  17.2 0.8 eq.88
  18.0 0.8 reshape.1587
  18.8 0.7 compare_convert_fusion
  19.6 0.7 bitcast_multiply_fusion
  20.4 6.6 %gather_fusion = f32[1024]{0:T(1024)S(1)} fusion(f32[19]{0:T(128)S(1)} %copy-done, s32[1024]{0:T(1024)S(1)} %broadcast_clamp_fusion.2), kind=kCustom, calls=%fused_computation | custom fusion | bytes 12288 | tf_op jit(solution)/shard_map/gather | solution.py:156
  27.1 6.6 %gather_fusion.1 = f32[1024]{0:T(1024)S(1)} fusion(f32[19]{0:T(128)S(1)} %copy-done.4, s32[1024]{0:T(1024)S(1)} %broadcast_clamp_fusion.2), kind=kCustom, calls=%fused_computation.1 | custom fusion | bytes 12288 | tf_op jit(solution)/shard_map/gather | solution.py:139
  33.8 6.6 %gather_fusion.3 = f32[1024]{0:T(1024)S(1)} fusion(f32[19]{0:T(128)S(1)} %copy-done.3, s32[1024]{0:T(1024)S(1)} %broadcast_clamp_fusion.2), kind=kCustom, calls=%fused_computation.3 | custom fusion | bytes 12288 | tf_op jit(solution)/shard_map/gather | solution.py:141
  40.4 6.6 %gather_fusion.4 = f32[1024]{0:T(1024)S(1)} fusion(f32[19]{0:T(128)S(1)} %copy-done.2, s32[1024]{0:T(1024)S(1)} %broadcast_clamp_fusion.2), kind=kCustom, calls=%fused_computation.4 | custom fusion | bytes 12288 | tf_op jit(solution)/shard_map/gather | solution.py:140
  47.0 0.6 scatter_custom_fusion.1
  47.7 0.6 scatter_custom_fusion.2
  48.6 0.6 gather_fusion.7
  49.2 0.6 gather_fusion.8
  49.8 2.7 %collective-permute-start.7 = (f32[19,18,8]{2,1,0:T(8,128)S(1)}, f32[19,18,8]{2,1,0:T(8,128)S(1)}, u32[]{:S(2)}, u32[]{:S(2)}) collective-permute-start(f32[19,18,8]{2,1,0:T(8,128)S(1)} %gather_fusion.8), channel_id=1, source_target_pairs={{1,0},{2,1},{3,2},{4,3},{5,4},{6,5},{7,6},{0,7},{9,8},{10,9},{11,1... | collective-permute-start | bytes 32840 | tf_op jit(solution)/shard_map/ppermute | solution.py:72
  52.6 2.6 %collective-permute-start.2 = (f32[26,3,1,64]{3,0,2,1:T(8,128)S(1)}, f32[26,3,1,64]{3,0,2,1:T(8,128)S(1)}, u32[]{:S(2)}, u32[]{:S(2)}) collective-permute-start(f32[26,3,1,64]{3,0,2,1:T(8,128)S(1)} %pad_maximum_fusion.10), channel_id=1, source_target_pairs={{1,0},{2,1},{3,2},{4,3},{5,4},{6,5},{7,6},{0,7},{9,8},{10,9},{11,1... | collective-permute-start | bytes 59912 | tf_op jit(solution)/shard_map/ppermute | solution.py:84
  55.8 1.5 %scatter_fusion.1 = f32[19,18,8]{1,2,0:T(8,128)S(1)} fusion(f32[19,18,8]{1,2,0:T(8,128)S(1)} %broadcast.889.clone, s32[19]{0:T(128)S(1)} %iota.60, f32[19,18,8]{1,2,0:T(8,128)S(1)} %copy.302), kind=kCustom, calls=%fused_computation.14 | custom fusion | bytes 32908 | tf_op jit(solution)/shard_map/scatter | solution.py:188
  57.7 1.5 %scatter_fusion.2 = f32[19,18,8]{1,2,0:T(8,128)S(1)} fusion(f32[19,18,8]{1,2,0:T(8,128)S(1)} %broadcast.889.clone.1, s32[19]{0:T(128)S(1)} %iota.66, f32[19,18,8]{1,2,0:T(8,128)S(1)} %copy.304), kind=kCustom, calls=%fused_computation.15 | custom fusion | bytes 32908 | tf_op jit(solution)/shard_map/scatter | solution.py:188
  60.9 2.8 %gather_fusion.2 = f32[1024,26]{1,0:T(8,128)S(1)} fusion(f32[26,320]{0,1:T(8,128)S(1)} %copy.293, s32[1024]{0:T(1024)S(1)} %get-tuple-element.62), kind=kCustom, calls=%fused_computation.2 | custom fusion | bytes 217088 | tf_op jit(solution)/shard_map/gather | solution.py:267
  64.1 0.6 scatter_fusion
  64.8 0.6 copy.296
  65.4 3.3 %all-to-all-start = ((f32[4,1,3,256]{3,1,2,0:T(1,128)}), f32[4,1,3,256]{3,1,2,0:T(1,128)S(1)}, u32[]{:S(2)}, u32[]{:S(2)}) async-start(f32[4,1,3,256]{3,1,2,0:T(1,128)} %copy.296), calls=%async_computation | async-start | bytes 24576 | tf_op jit(solution)/shard_map/all_to_all | solution.py:296
  68.7 0.7 scatter_fusion.3
  69.4 1.0 copy.307
  70.4 0.7 copy.336
  71.0 3.2 %all-to-all-done = f32[4,1,3,256]{3,1,2,0:T(1,128)S(1)} async-done(((f32[4,1,3,256]{3,1,2,0:T(1,128)}), f32[4,1,3,256]{3,1,2,0:T(1,128)S(1)}, u32[]{:S(2)}, u32[]{:S(2)}) %all-to-all-start) | async-done | bytes 12320 | tf_op jit(solution)/shard_map/all_to_all | solution.py:296
  74.2 3.6 %all-to-all-start.1 = ((f32[4,1,19,800]{3,1,2,0:T(1,128)}), f32[4,1,19,800]{3,1,2,0:T(1,128)S(1)}, u32[]{:S(2)}, u32[]{:S(2)}) async-start(f32[4,1,19,800]{3,1,2,0:T(1,128)} %copy.307), calls=%async_computation.1 | async-start | bytes 544768 | tf_op jit(solution)/shard_map/all_to_all | solution.py:295
  78.0 6.6 %gather_fusion.9 = s32[1024]{0:T(1024)S(1)} fusion(s32[19]{0:T(128)S(1)} %copy-done.1, s32[1024]{0:T(1024)S(1)} %broadcast_clamp_fusion.1), kind=kCustom, calls=%fused_computation.9 | custom fusion | bytes 12288 | tf_op jit(solution)/shard_map/vmap()/gather | solution.py:227
  84.9 2.4 %all-to-all-done.1 = f32[4,1,19,800]{3,1,2,0:T(1,128)S(1)} async-done(((f32[4,1,19,800]{3,1,2,0:T(1,128)}), f32[4,1,19,800]{3,1,2,0:T(1,128)S(1)}, u32[]{:S(2)}, u32[]{:S(2)}) %all-to-all-start.1) | async-done | bytes 243232 | tf_op jit(solution)/shard_map/all_to_all | solution.py:295
  88.2 0.6 fusion.5
  91.9 1.1 slice.734
  93.0 3.6 %copy.335 = f32[4,19,8,8,8]{4,3,2,1,0:T(8,128)S(1)} copy(f32[4,19,8,8,8]{1,4,3,2,0:T(8,128)} %slice.734) | data formatting | bytes 311296 | tf_op jit(solution)/shard_map/vmap()/slice | solution.py:217
  96.6 1.3 %reshape.1596 = f32[4,9728]{1,0:T(4,128)S(1)} reshape(f32[4,19,8,8,8]{4,3,2,1,0:T(8,128)S(1)} %copy.335) | data formatting | bytes 311296 | tf_op jit(solution)/shard_map/vmap()/reshape | solution.py:217
  98.0 9.2 %gather_fusion.10 = f32[1024]{0:T(1024)S(1)} fusion(f32[4,9728]{1,0:T(4,128)S(1)} %reshape.1596, s32[1024]{0:T(1024)S(1)} %bitcast.459), kind=kCustom, calls=%fused_computation.10 | custom fusion | bytes 16384 | tf_op jit(solution)/shard_map/vmap()/gather | solution.py:228
  109.3 1.1 slice.732
  110.5 3.6 %copy.333 = f32[4,19,8,8,8]{4,3,2,1,0:T(8,128)S(1)} copy(f32[4,19,8,8,8]{1,4,3,2,0:T(8,128)} %slice.732) | data formatting | bytes 311296 | tf_op jit(solution)/shard_map/vmap()/slice | solution.py:217
  114.1 1.2 %reshape.1599 = f32[38912]{0:T(1024)S(1)} reshape(f32[4,19,8,8,8]{4,3,2,1,0:T(8,128)S(1)} %copy.333) | data formatting | bytes 311296
  115.3 4.4 %scatter_fusion.4 = f32[38912]{0:T(1024)S(1)} fusion(f32[38912]{0:T(1024)S(1)} %reshape.1599, s32[1024]{0:T(1024)S(1)} %bitcast.538, f32[1024]{0:T(1024)S(1)} %bitcast.539), kind=kCustom, calls=%fused_computation.17 | custom fusion | bytes 16384
  119.9 0.9 reshape.1597
  (222 shorter events, 11.7 us)
Async XLA Ops:
  0.6 19.8 %copy-start = (f32[19]{0:T(128)S(1)}, f32[19]{0:T(128)}, u32[]{:S(2)}) copy-start(f32[19]{0:T(128)} %constant.188.clone) | copy-start | bytes 232
  1.3 25.8 %copy-start.4 = (f32[19]{0:T(128)S(1)}, f32[19]{0:T(128)}, u32[]{:S(2)}) copy-start(f32[19]{0:T(128)} %constant.204) | copy-start | bytes 232
  5.3 47.2 %collective-permute-start = (f32[26,1,1,64]{3,0,2,1:T(8,128)S(1)}, f32[26,1,1,64]{3,0,2,1:T(8,128)S(1)}, u32[]{:S(2)}, u32[]{:S(2)}) collective-permute-start(f32[26,1,1,64]{3,0,2,1:T(8,128)S(1)} %convolution_bitcast_fusion.1), channel_id=1, source_target_pairs={{0,8},{8,16},{16,24},{24,0},{1,9},{9,17},{17,25},{25,1},{2,10},{10... | collective-permute-start | bytes 19976 | tf_op jit(solution)/shard_map/ppermute | solution.py:81
  8.4 44.1 %collective-permute-start.1 = (f32[26,1,1,64]{3,0,2,1:T(8,128)S(1)}, f32[26,1,1,64]{3,0,2,1:T(8,128)S(1)}, u32[]{:S(2)}, u32[]{:S(2)}) collective-permute-start(f32[26,1,1,64]{3,0,2,1:T(8,128)S(1)} %convolution_bitcast_fusion.1), channel_id=1, source_target_pairs={{8,0},{16,8},{24,16},{0,24},{9,1},{17,9},{25,17},{1,25},{10,2},{18... | collective-permute-start | bytes 19976 | tf_op jit(solution)/shard_map/ppermute | solution.py:84
  12.8 34.3 %collective-permute-start.4 = (f32[19,1,128]{2,0,1:T(8,128)S(1)}, f32[19,1,128]{2,0,1:T(8,128)S(1)}, u32[]{:S(2)}, u32[]{:S(2)}) collective-permute-start(f32[19,1,128]{2,0,1:T(8,128)S(1)} %bitcast.549), channel_id=1, source_target_pairs={{24,0},{0,8},{8,16},{16,24},{25,1},{1,9},{9,17},{17,25},{26,2},{2,... | collective-permute-start | bytes 29192 | tf_op jit(solution)/shard_map/ppermute | solution.py:72
  13.4 34.3 %collective-permute-start.5 = (f32[19,1,128]{2,0,1:T(8,128)S(1)}, f32[19,1,128]{2,0,1:T(8,128)S(1)}, u32[]{:S(2)}, u32[]{:S(2)}) collective-permute-start(f32[19,1,128]{2,0,1:T(8,128)S(1)} %bitcast.548), channel_id=1, source_target_pairs={{8,0},{16,8},{24,16},{0,24},{9,1},{17,9},{25,17},{1,25},{10,2},{18... | collective-permute-start | bytes 29192 | tf_op jit(solution)/shard_map/ppermute | solution.py:72
  27.0 6.7 %copy-start.3 = (f32[19]{0:T(128)S(1)}, f32[19]{0:T(128)}, u32[]{:S(2)}) copy-start(f32[19]{0:T(128)} %constant.206) | copy-start | bytes 232
  33.7 6.6 %copy-start.2 = (f32[19]{0:T(128)S(1)}, f32[19]{0:T(128)}, u32[]{:S(2)}) copy-start(f32[19]{0:T(128)} %constant.208) | copy-start | bytes 232
  40.3 8.0 %copy-start.5 = (f32[19,16,128]{2,1,0:T(8,128)S(1)}, f32[19,16,128]{2,1,0:T(8,128)}, u32[]{:S(2)}) copy-start(f32[19,16,128]{2,1,0:T(8,128)} %param.18) | copy-start | bytes 466948
  49.2 6.4 %collective-permute-start.6 = (f32[19,18,8]{2,1,0:T(8,128)S(1)}, f32[19,18,8]{2,1,0:T(8,128)S(1)}, u32[]{:S(2)}, u32[]{:S(2)}) collective-permute-start(f32[19,18,8]{2,1,0:T(8,128)S(1)} %gather_fusion.7), channel_id=1, source_target_pairs={{7,0},{0,1},{1,2},{2,3},{3,4},{4,5},{5,6},{6,7},{15,8},{8,9},{9,10... | collective-permute-start | bytes 32840 | tf_op jit(solution)/shard_map/ppermute | solution.py:72
  49.8 7.7 %collective-permute-start.7 = (f32[19,18,8]{2,1,0:T(8,128)S(1)}, f32[19,18,8]{2,1,0:T(8,128)S(1)}, u32[]{:S(2)}, u32[]{:S(2)}) collective-permute-start(f32[19,18,8]{2,1,0:T(8,128)S(1)} %gather_fusion.8), channel_id=1, source_target_pairs={{1,0},{2,1},{3,2},{4,3},{5,4},{6,5},{7,6},{0,7},{9,8},{10,9},{11,1... | collective-permute-start | bytes 32840 | tf_op jit(solution)/shard_map/ppermute | solution.py:72
  52.5 7.8 %collective-permute-start.3 = (f32[26,3,1,64]{3,0,2,1:T(8,128)S(1)}, f32[26,3,1,64]{3,0,2,1:T(8,128)S(1)}, u32[]{:S(2)}, u32[]{:S(2)}) collective-permute-start(f32[26,3,1,64]{3,0,2,1:T(8,128)S(1)} %pad_maximum_fusion.10), channel_id=1, source_target_pairs={{0,1},{1,2},{2,3},{3,4},{4,5},{5,6},{6,7},{7,0},{8,9},{9,10},{10,1... | collective-permute-start | bytes 59912 | tf_op jit(solution)/shard_map/ppermute | solution.py:81
  52.6 7.8 %collective-permute-start.2 = (f32[26,3,1,64]{3,0,2,1:T(8,128)S(1)}, f32[26,3,1,64]{3,0,2,1:T(8,128)S(1)}, u32[]{:S(2)}, u32[]{:S(2)}) collective-permute-start(f32[26,3,1,64]{3,0,2,1:T(8,128)S(1)} %pad_maximum_fusion.10), channel_id=1, source_target_pairs={{1,0},{2,1},{3,2},{4,3},{5,4},{6,5},{7,6},{0,7},{9,8},{10,9},{11,1... | collective-permute-start | bytes 59912 | tf_op jit(solution)/shard_map/ppermute | solution.py:84
  60.9 17.0 %copy-start.1 = (s32[19]{0:T(128)S(1)}, s32[19]{0:T(128)}, u32[]{:S(2)}) copy-start(s32[19]{0:T(128)} %constant.191.clone) | copy-start | bytes 232
  65.4 8.8 %all-to-all-start = ((f32[4,1,3,256]{3,1,2,0:T(1,128)}), f32[4,1,3,256]{3,1,2,0:T(1,128)S(1)}, u32[]{:S(2)}, u32[]{:S(2)}) async-start(f32[4,1,3,256]{3,1,2,0:T(1,128)} %copy.296), calls=%async_computation | async-start | bytes 24576 | tf_op jit(solution)/shard_map/all_to_all | solution.py:296
  70.4 14.2 %copy-start.8 = (s32[2]{0:T(128)S(1)}, s32[2]{0:T(128)}, u32[]{:S(2)}) copy-start(s32[2]{0:T(128)} %constant.196) | copy-start | bytes 28
  70.4 14.3 %copy-start.7 = (s32[2]{0:T(128)S(1)}, s32[2]{0:T(128)}, u32[]{:S(2)}) copy-start(s32[2]{0:T(128)} %constant.199) | copy-start | bytes 28
  74.2 13.1 %all-to-all-start.1 = ((f32[4,1,19,800]{3,1,2,0:T(1,128)}), f32[4,1,19,800]{3,1,2,0:T(1,128)S(1)}, u32[]{:S(2)}, u32[]{:S(2)}) async-start(f32[4,1,19,800]{3,1,2,0:T(1,128)} %copy.307), calls=%async_computation.1 | async-start | bytes 544768 | tf_op jit(solution)/shard_map/all_to_all | solution.py:295
  77.8 9.5 %copy-start.6 = (f32[10,19,1]{1,0,2:T(8,128)S(1)}, f32[10,19,1]{1,0,2:T(8,128)}, u32[]{:S(2)}) copy-start(f32[10,19,1]{1,0,2:T(8,128)} %constant.223) | copy-start | bytes 2284
  77.9 10.3 %copy-start.9 = (f32[19,3,1]{0,1,2:T(4,128)S(1)}, f32[19,3,1]{0,1,2:T(4,128)}, u32[]{:S(2)}) copy-start(f32[19,3,1]{0,1,2:T(4,128)} %constant.224) | copy-start | bytes 688
where the time goes:
time: 121 us
  local copies, waits for them, and re-layouts  81.3 us (67%)
  starting transfers between devices  21.4 us (18%)
  other arithmetic  8.73 us (7%)
  waiting for transfers between devices  5.8 us (5%)
  matrix products  2 us (2%)
  between operations  1.59 us (1%)
    slice x4, local copies, waits for them, and re-layouts, interior_of(): flat_tile.reshape(Q, E + 2, E + 2, Z)[:, 1:E + 1, 1:E + 1, :]  9.51 us
    gather x2, local copies, waits for them, and re-layouts, finish_tile(): values = interior[codes_int] - extra_rows[0]  9.17 us
    ppermute x4, starting transfers between devices, shifted(): return lax.ppermute(block, axis, route)  6.66 us
    gather x2, local copies, waits for them, and re-layouts, link_correction(): step_x = vel_table[:, 0][direction_ids]  6.58 us
    gather x2, local copies, waits for them, and re-layouts, link_correction(): step_z = vel_table[:, 2][direction_ids]  6.58 us
    gather x2, local copies, waits for them, and re-layouts, link_correction(): step_y = vel_table[:, 1][direction_ids]  6.58 us
    gather x1, local copies, waits for them, and re-layouts, link_correction(): jnp.asarray(lattice_wts)[direction_ids]  6.57 us
    gather x1, local copies, waits for them, and re-layouts, finish_tile(): target = jnp.asarray(opposite_dir)[codes_int // CB] * CB + codes_int % CB  6.57 us
  transfers between devices with their start and end apart: 10, of which 3 were waited for; matrix products, arithmetic and copies ran while one was open for 41% of the time, Pallas kernels for 0%

commit v1 on v0

v1 whole, which is shorter than its diff:
```python
import functools

import jax
import jax.numpy as jnp
import numpy as np
from jax import lax
from jax.experimental import pallas as pl
from jax.experimental.pallas import tpu as pltpu
from jax.sharding import PartitionSpec as P

MESH = pl.DeviceIdType.MESH
F32 = jnp.float32
BF16 = jnp.bfloat16

vel = [
    (0, 0, 0), (1, 0, 0), (-1, 0, 0), (0, 1, 0), (0, -1, 0), (0, 0, 1), (0, 0, -1),
    (1, 1, 0), (-1, -1, 0), (1, -1, 0), (-1, 1, 0),
    (1, 0, 1), (-1, 0, -1), (1, 0, -1), (-1, 0, 1),
    (0, 1, 1), (0, -1, -1), (0, 1, -1), (0, -1, 1),
]
opp = [0, 2, 1, 4, 3, 6, 5, 8, 7, 10, 9, 12, 11, 14, 13, 16, 15, 18, 17]
wts = [1.0 / 3.0] + [1.0 / 18.0] * 6 + [1.0 / 36.0] * 12
codes = (0, 1, 2, 3, 5, 6, 7, 8)
plus_x = [q for q in range(19) if vel[q][0] == 1]
minus_x = [q for q in range(19) if vel[q][0] == -1]
plus_y = [q for q in range(19) if vel[q][1] == 1]
minus_y = [q for q in range(19) if vel[q][1] == -1]
corner_dir = {(1, 1): 7, (-1, -1): 8, (1, -1): 9, (-1, 1): 10}


def steps_of(code):
    return code // 3 - 1, code % 3 - 1


def rows_of(code):
    dx, dy = steps_of(code)
    return 24 if dx == 0 else 16 if dy == 0 else 8


def roll(value, shift, axis):
    size = value.shape[axis]
    shift = shift % size
    return value if shift == 0 else pltpu.roll(value, shift, axis)


def split3(value):
    high = value.astype(BF16)
    rest = value - high.astype(F32)
    mid = rest.astype(BF16)
    low = (rest - mid.astype(F32)).astype(BF16)
    return high, mid, low


def collide(load):
    f = [load(q) for q in range(19)]
    sx = [f[q] for q in plus_x]
    density = functools.reduce(lambda a, b: a + b, f)

    def total(qs):
        return functools.reduce(lambda a, b: a + b, [f[q] for q in qs])

    px, mx = total(plus_x), total(minus_x)
    py, my = total(plus_y), total(minus_y)
    plus_z = [q for q in range(19) if vel[q][2] == 1]
    minus_z = [q for q in range(19) if vel[q][2] == -1]
    pz, mz = total(plus_z), total(minus_z)
    inverse = 1.0 / density
    ux, uy, uz = (px - mx) * inverse, (py - my) * inverse, (pz - mz) * inverse
    third = density * (1.0 / 3.0)
    dux, duy, duz = density * ux, density * uy, density * uz
    xx = (px + mx) - third - dux * ux
    yy = (py + my) - third - duy * uy
    zz = (pz + mz) - third - duz * uz
    xy = (f[7] + f[8]) - (f[9] + f[10]) - dux * uy
    xz = (f[11] + f[12]) - (f[13] + f[14]) - dux * uz
    yz = (f[15] + f[16]) - (f[17] + f[18]) - duy * uz
    contracted = xx * xx + yy * yy + zz * zz + 2.0 * (xy * xy + xz * xz + yz * yz)
    shear = (1.5 / 0.8) * inverse * jnp.sqrt(2.0 * contracted)
    scaled = 20.0 * shear
    viscosity = 0.01 + (0.1 - 0.01) * lax.rsqrt(jnp.sqrt(1.0 + scaled * scaled))
    omega = 1.0 / (3.0 * viscosity + 0.5)
    base = 1.0 - 1.5 * (ux * ux + uy * uy + uz * uz)
    keep = 1.0 - omega
    gain = {w: omega * density * w for w in set(wts)}
    out = []
    for q in range(19):
        c = None
        for step, u in zip(vel[q], (ux, uy, uz)):
            if step:
                term = u if step > 0 else -u
                c = term if c is None else c + term
        bracket = base if c is None else base + c * (3.0 + 4.5 * c)
        out.append(keep * f[q] + gain[wts[q]] * bracket)
    return out


def kernel(nx, ny, pdf_ref, grains_ref, moves_ref, owner_ref, links_ref,
           blocks_ref, table_ref,
           star, zstar, final, pad, tab, outbox, inbox, parcel,
           note_send, note_recv, block_send, block_recv, local_sem):
    gx = lax.axis_index("gx")
    gy = lax.axis_index("gy")

    def device(dx, dy):
        return (lax.rem(gx + dx + nx, nx), lax.rem(gy + dy + ny, ny))

    barrier = pltpu.get_barrier_semaphore()
    peers = [steps_of(m) for m in codes] + [(d, 0) for d in range(2, nx - 1)]
    for dx, dy in peers:
        pl.semaphore_signal(barrier, inc=1, device_id=device(dx, dy), device_id_type=MESH)

    lane = lax.broadcasted_iota(jnp.int32, (16, 128), 1)
    row = lax.broadcasted_iota(jnp.int32, (16, 128), 0)
    depth = lane % 8

    pad[...] = jnp.zeros_like(pad)
    own = grains_ref[:, 0, :]
    pad[0:26, :] = own
    code = moves_ref[...]
    kind = lax.broadcasted_iota(jnp.int32, (16, 256), 0)
    match = jnp.where(kind == code, 1.0, 0.0)
    before = jnp.where(
        lax.broadcasted_iota(jnp.int32, (256, 256), 0)
        < lax.broadcasted_iota(jnp.int32, (256, 256), 1), 1.0, 0.0)
    counts = jnp.dot(match.astype(BF16), before.astype(BF16), preferred_element_type=F32)
    rank = jnp.sum(match * counts, axis=0, keepdims=True).astype(jnp.int32)
    region = jnp.where(code > 4, code - 1, code)
    target = jnp.where(code == 4, -1, region * 8 + rank)
    slot = lax.broadcasted_iota(jnp.int32, (64, 256), 0)
    placing = jnp.where(slot == target, 1.0, 0.0).astype(BF16)
    parts = jnp.concatenate(list(split3(pad[...])) + [jnp.zeros((32, 256), BF16)], axis=0)
    packed = lax.dot_general(placing, parts, (((1,), (1,)), ((), ())),
                             preferred_element_type=F32)
    packed = packed + roll(packed, -32, 1) + roll(packed, -64, 1)
    packed = jnp.where(lax.broadcasted_iota(jnp.int32, (64, 128), 1) < 32, packed, 0.0)

    collided = collide(lambda q: pdf_ref[q])
    for q in range(19):
        star[q] = collided[q]
        shifted = collided[q]
        if vel[q][2] == 1:
            shifted = jnp.where(depth == 0, roll(shifted, -7, 1), roll(shifted, 1, 1))
        elif vel[q][2] == -1:
            shifted = jnp.where(depth == 7, roll(shifted, 7, 1), roll(shifted, -1, 1))
        zstar[q] = shifted

    for k, m in enumerate(codes):
        dx, dy = steps_of(m)
        tile = packed[k * 8:(k + 1) * 8, :]
        if dx and dy:
            edge = zstar[corner_dir[dx, dy], pl.ds(15 if dx == 1 else 0, 1), :]
            if dy == -1:
                edge = roll(jnp.broadcast_to(edge, (8, 128)), 120, 1)
            tile = jnp.where(lane[0:8] >= 120, edge, tile)
        outbox[k, 0:8, :] = tile
        if dy == 0:
            for i, q in enumerate(plus_x if dx == 1 else minus_x):
                outbox[k, 8 + i:9 + i, :] = zstar[q, pl.ds(15 if dx == 1 else 0, 1), :]
        elif dx == 0:
            face = jnp.zeros((16, 128), F32)
            for i, q in enumerate(plus_y if dy == 1 else minus_y):
                moved = roll(zstar[q], 8 * i + (8 if dy == 1 else 0), 1)
                face = jnp.where(lane // 8 == i, moved, face)
            outbox[k, 8:24, :] = face

    pl.semaphore_wait(barrier, len(peers))
    notes = []
    for k, m in enumerate(codes):
        copy = pltpu.make_async_remote_copy(
            src_ref=outbox.at[k, pl.ds(0, rows_of(m))],
            dst_ref=inbox.at[k, pl.ds(0, rows_of(m))],
            send_sem=note_send.at[k], recv_sem=note_recv.at[k],
            device_id=device(*steps_of(m)), device_id_type=MESH)
        copy.start()
        notes.append(copy)

    kept = own * jnp.where(code == 4, 1.0, 0.0)
    tab[...] = jnp.zeros_like(tab)
    tab[0:26, 0:256] = kept
    cells, dirs, slots = links_ref[0], links_ref[1], links_ref[2]

    def step_along(axis):
        value = jnp.zeros((2, 512), F32)
        for q in range(1, 19):
            if vel[q][axis]:
                value = jnp.where(dirs == q, float(vel[q][axis]), value)
        return value

    step_x, step_y, step_z = step_along(0), step_along(1), step_along(2)
    half = lax.broadcasted_iota(jnp.int32, (2, 512), 1) // 256
    bx = lax.broadcasted_iota(jnp.int32, (2, 512), 0)
    cell_x, cell_y, cell_z = cells // 64, cells // 8 % 8, cells % 8
    mid_x = ((gx * 2 + bx) * 8 + cell_x).astype(F32) + 0.5 * step_x
    mid_y = ((gy * 2 + half) * 8 + cell_y).astype(F32) + 0.5 * step_y
    mid_z = cell_z.astype(F32) + 0.5 * step_z
    scale = jnp.where(dirs < 7, 6.0 / 18.0, 6.0 / 36.0)
    place = half * 64 + cells % 64
    fdirs = dirs.astype(F32)

    for copy in notes:
        copy.wait()

    incoming = inbox[:, 0:8, :].reshape(64, 128)
    incoming = jnp.concatenate([incoming, jnp.zeros((64, 128), F32)], axis=0).T
    tab[0:26, 256:384] = incoming[0:26, :]
    table_ref[...] = tab[0:26, 0:320]
    features = jnp.concatenate(list(split3(tab[0:16, :])), axis=0)
    dense = []
    for b in range(2):
        def at(value):
            return value[b:b + 1, :]

        chosen = jnp.where(
            lax.broadcasted_iota(jnp.int32, (384, 512), 0) == at(slots), 1.0, 0.0).astype(BF16)
        g = jnp.dot(features, chosen, preferred_element_type=F32)
        g = g[0:16] + g[16:32] + g[32:48]
        rel_x, rel_y, rel_z = at(mid_x) - g[0:1], at(mid_y) - g[1:2], at(mid_z) - g[2:3]
        wall_x = g[3:4] + g[7:8] * rel_z - g[8:9] * rel_y
        wall_y = g[4:5] + g[8:9] * rel_x - g[6:7] * rel_z
        wall_z = g[5:6] + g[6:7] * rel_y - g[7:8] * rel_x
        correction = at(scale) * (
            at(step_x) * wall_x + at(step_y) * wall_y + at(step_z) * wall_z)
        in_row = lax.broadcasted_iota(jnp.int32, (8, 512), 0) == at(cell_x)
        values = [p.astype(F32) for p in split3(correction)] + [at(fdirs)]
        spread = jnp.concatenate(
            [jnp.where(in_row, value, 0.0) for value in values], axis=0).astype(BF16)
        where_to = jnp.where(
            lax.broadcasted_iota(jnp.int32, (128, 512), 0) == at(place), 1.0, 0.0).astype(BF16)
        dense.append(lax.dot_general(spread, where_to, (((1,), (1,)), ((), ())),
                                     preferred_element_type=F32))
    correction = jnp.concatenate([d[0:8] + d[8:16] + d[16:24] for d in dense], axis=0)
    link_dir = jnp.concatenate([d[24:32] for d in dense], axis=0)

    region_of = {steps_of(m): k for k, m in enumerate(codes)}
    for q in range(19):
        sx, sy, _ = vel[q]
        value = zstar[q]
        edge_lane = lane < 8 if sy == 1 else lane >= 120
        if sy:
            i = (plus_y if sy == 1 else minus_y).index(q)
            ghost = inbox[region_of[0, sy], 8:24, :]
            ghost = roll(ghost, -8 * i + (0 if sy == 1 else 120), 1)
            value = jnp.where(edge_lane, ghost, roll(value, 8 * sy, 1))
        if sx:
            i = (plus_x if sx == 1 else minus_x).index(q)
            line = inbox[region_of[sx, 0], 8 + i:9 + i, :]
            if sy:
                line = roll(jnp.broadcast_to(line, (8, 128)), 8 * sy, 1)
                corner = inbox[region_of[sx, sy], 0:8, :]
                corner = roll(corner, 8, 1) if sy == 1 else corner
                line = jnp.where(edge_lane[0:8], corner, line)[0:1]
            value = jnp.where(row == (0 if sx == 1 else 15), line, roll(value, sx, 0))
        if q:
            value = jnp.where(link_dir == float(opp[q]), star[opp[q]] - correction, value)
        final[q * 16:(q + 1) * 16, :] = value

    wide = lax.broadcasted_iota(jnp.int32, (24, 128), 1) < 64
    holds = [jnp.full((24, 128), owner_ref[n // 2, n % 2], jnp.int32) for n in range(4)]
    for k in range(4):
        pieces = []
        for b in range(2):
            first = final[pl.ds(b * 8 + 2 * k, 24, stride=16), :]
            second = final[pl.ds(b * 8 + 2 * k + 1, 24, stride=16), :]
            pieces.append(jnp.where(wide, first, roll(second, 64, 1)))
            pieces.append(jnp.where(wide, roll(first, 64, 1), second))
        for o in range(nx):
            value = jnp.zeros((24, 128), F32)
            for n in range(4):
                value = jnp.where(holds[n] == o, pieces[n], value)
            parcel[o, :, k * 128:(k + 1) * 128] = value[0:19]

    sends = []
    for d in range(1, nx):
        to = lax.rem(gx + d, nx)
        copy = pltpu.make_async_remote_copy(
            src_ref=parcel.at[to], dst_ref=blocks_ref.at[gx],
            send_sem=block_send.at[d - 1], recv_sem=block_recv.at[d - 1],
            device_id=(to, gy), device_id_type=MESH)
        copy.start()
        sends.append(copy)
    here = pltpu.make_async_copy(parcel.at[gx], blocks_ref.at[gx], local_sem)
    here.start()
    here.wait()
    for copy in sends:
        copy.wait()


def body(pdf, grains, grain_moves, owner_map, link_lists):
    nx, ny = lax.axis_size("gx"), lax.axis_size("gy")
    vmem = pl.BlockSpec(memory_space=pltpu.VMEM)
    blocks, table = pl.pallas_call(
        functools.partial(kernel, nx, ny),
        out_shape=(jax.ShapeDtypeStruct((nx, 19, 512), F32),
                   jax.ShapeDtypeStruct((26, 320), F32)),
        in_specs=[vmem, vmem, vmem, pl.BlockSpec(memory_space=pltpu.SMEM), vmem],
        out_specs=(pl.BlockSpec(memory_space=pl.ANY), vmem),
        scratch_shapes=[
            pltpu.VMEM((19, 16, 128), F32),
            pltpu.VMEM((19, 16, 128), F32),
            pltpu.VMEM((384, 128), F32),
            pltpu.VMEM((32, 256), F32),
            pltpu.VMEM((32, 384), F32),
            pltpu.VMEM((8, 24, 128), F32),
            pltpu.VMEM((8, 24, 128), F32),
            pltpu.VMEM((nx, 19, 512), F32),
            pltpu.SemaphoreType.DMA((8,)),
            pltpu.SemaphoreType.DMA((8,)),
            pltpu.SemaphoreType.DMA((nx - 1,)),
            pltpu.SemaphoreType.DMA((nx - 1,)),
            pltpu.SemaphoreType.DMA,
        ],
        compiler_params=pltpu.CompilerParams(
            collective_id=0, has_side_effects=True, vmem_limit_bytes=32 * 1024 * 1024),
        name="slab_step",
    )(pdf, grains, grain_moves, owner_map, link_lists)
    return blocks[:, None], table[:, None, :]


def solution(mesh):
    in_specs = (
        P(None, "gx", "gy"),
        P(None, "gx", "gy"),
        P("gx", "gy"),
        P("gx", "gy"),
        P(None, "gx", "gy"),
    )
    out_specs = (P("gx", "gy", None, None), P(None, "gx", "gy"))
    return jax.shard_map(body, mesh=mesh, in_specs=in_specs, out_specs=out_specs, check_vma=False)
```

time: 121 us -> 22.1 us (0.18)
  local copies, waits for them, and re-layouts: 81.3 us -> 5.19 us
  starting transfers between devices: 21.4 us -> 0 us
  Pallas kernels: 0 us -> 15.9 us
  other arithmetic: 8.73 us -> 0 us
  waiting for transfers between devices: 5.8 us -> 0 us
  matrix products: 2 us -> 0 us
    gather x16 -> x0, local copies, waits for them, and re-layouts: 47.3 us -> none  [the longest x2 9.17 us: finish_tile(): values = interior[codes_int] - extra_rows[0]]
    pallas_call x0 -> x1, Pallas kernels: none -> 15.9 us  [body(): pl.pallas_call(functools.partial(kernel, nx, ny), out_shape=(jax.ShapeDty...]
    ppermute x8 -> x0, starting transfers between devices: 14.5 us -> none  [the longest x4 6.66 us: shifted(): return lax.ppermute(block, axis, route)]
    slice x32 -> x0, local copies, waits for them, and re-layouts: 12 us -> none  [the longest x4 9.51 us: interior_of(): flat_tile.reshape(Q, E + 2, E + 2, Z)[:, 1:E + 1, 1:E + 1, :]]
    all_to_all x2 -> x0, starting transfers between devices: 6.88 us -> none  [the longest x1 3.63 us: body(): lax.all_to_all(send_tiles, 'gx', split_axis=0, concat_axis=0, tiled=True)]
    scatter x11 -> x0, local copies, waits for them, and re-layouts: 6.08 us -> none  [the longest x4 3.42 us: extend(): jnp.zeros((count_dirs, widened.shape[1], Z), widened.dtype).at[chosen]]
    all_to_all x2 -> x0, waiting for transfers between devices: 5.53 us -> none  [the longest x1 3.16 us: body(): lax.all_to_all(send_extras, 'gx', split_axis=0, concat_axis=0, tiled=True)]
    reshape x5 -> x0, local copies, waits for them, and re-layouts: 4.55 us -> none  [the longest x1 1.32 us: interior_of(): flat_tile.reshape(Q, E + 2, E + 2, Z)[:, 1:E + 1, 1:E + 1, :]]
  transfers between devices with their start and end apart: 10 -> 0, of which waited for: 3 -> 0; matrix products, arithmetic and copies ran while one was open for 41% -> 0% of each run, Pallas kernels for 0% -> 0%
where the time goes in v1:
time: 22.1 us; the launch traced here: 21.8 us
  Pallas kernels  15.9 us (72%)
  local copies, waits for them, and re-layouts  5.19 us (23%)
  between operations  0.65 us (3%)
    pallas_call x1, Pallas kernels, body(): pl.pallas_call(functools.partial(kernel, nx, ny), out_shape=(jax.ShapeDty...  15.9 us
    unnamed x12, local copies, waits for them, and re-layouts  5.19 us

profile of v1, /device:TPU:0, one launch (start us, length us, event | category | flops | bytes accessed | tf_op | source)
XLA Modules:
  0.0 21.8 jit_solution(9663025566961991836)
XLA Ops:
  0.6 0.0 copy-start
  0.6 0.9 %copy-done = f32[19,16,128]{2,1,0:T(8,128)S(1)} copy-done((f32[19,16,128]{2,1,0:T(8,128)S(1)}, f32[19,16,128]{2,1,0:T(8,128)}, u32[]{:S(2)}) %copy-start) | copy-done | bytes 155672
  1.5 0.0 copy-start.1
  1.5 0.7 %copy-done.1 = f32[26,1,256]{2,1,0:T(1,128)S(1)} copy-done((f32[26,1,256]{2,1,0:T(1,128)S(1)}, f32[26,1,256]{2,1,0:T(1,128)}, u32[]{:S(2)}) %copy-start.1) | copy-done | bytes 26648
  2.3 0.0 copy-start.2
  2.3 0.7 %copy-done.2 = s32[3,2,512]{2,1,0:T(2,128)S(1)} copy-done((s32[3,2,512]{2,1,0:T(2,128)S(1)}, s32[3,2,512]{2,1,0:T(2,128)}, u32[]{:S(2)}) %copy-start.2) | copy-done | bytes 12312
  3.0 0.0 copy-start.3
  3.0 0.7 %copy-done.3 = s32[1,256]{1,0:T(1,128)S(1)} copy-done((s32[1,256]{1,0:T(1,128)S(1)}, s32[1,256]{1,0:T(1,128)}, u32[]{:S(2)}) %copy-start.3) | copy-done | bytes 1048
  3.7 0.0 copy-start.4
  3.7 0.7 %copy-done.4 = s32[2,2]{1,0:T(2,128)S(1)} copy-done((s32[2,2]{1,0:T(2,128)S(1)}, s32[2,2]{1,0:T(2,128)}, u32[]{:S(2)}) %copy-start.4) | copy-done | bytes 40
  4.4 15.9 %slab_step.1 = (f32[4,19,512]{2,1,0:T(8,128)S(1)}, f32[26,320]{1,0:T(8,128)S(1)}) custom-call(f32[19,16,128]{2,1,0:T(8,128)S(1)} %copy-done, f32[26,1,256]{2,1,0:T(1,128)S(1)} %copy-done.1, s32[1,256]{1,0:T(1,128)S(1)} %copy-done.3, s32[2,2]{1,0:T(2,128)S(1)} %copy-done.4, s32[3,2,512]{2,1,0:T(2,128)S(1)} %copy-done.2), custom_call_target="tpu_custom_call" | custom-call | tf_op jit(solution)/shard_map/slab_step/pallas_call | solution.py:291
  20.3 0.8 %copy.7 = f32[4,1,19,512]{3,1,2,0:T(1,128)} copy(f32[4,1,19,512]{3,2,0,1:T(8,128)S(1)} %bitcast.2) | data formatting | bytes 311296
  21.1 0.7 %copy.8 = f32[26,1,320]{2,1,0:T(1,128)} copy(f32[26,1,320]{2,0,1:T(8,128)S(1)} %bitcast.3) | data formatting | bytes 66560
Async XLA Ops:
  0.6 0.9 %copy-start = (f32[19,16,128]{2,1,0:T(8,128)S(1)}, f32[19,16,128]{2,1,0:T(8,128)}, u32[]{:S(2)}) copy-start(f32[19,16,128]{2,1,0:T(8,128)} %pdf_ref.1) | copy-start | bytes 466948
  1.5 0.7 %copy-start.1 = (f32[26,1,256]{2,1,0:T(1,128)S(1)}, f32[26,1,256]{2,1,0:T(1,128)}, u32[]{:S(2)}) copy-start(f32[26,1,256]{2,1,0:T(1,128)} %grains_ref.1) | copy-start | bytes 79876
  2.3 0.7 %copy-start.2 = (s32[3,2,512]{2,1,0:T(2,128)S(1)}, s32[3,2,512]{2,1,0:T(2,128)}, u32[]{:S(2)}) copy-start(s32[3,2,512]{2,1,0:T(2,128)} %links_ref.1) | copy-start | bytes 36868
  3.0 0.7 %copy-start.3 = (s32[1,256]{1,0:T(1,128)S(1)}, s32[1,256]{1,0:T(1,128)}, u32[]{:S(2)}) copy-start(s32[1,256]{1,0:T(1,128)} %moves_ref.1) | copy-start | bytes 3076
  3.7 0.7 %copy-start.4 = (s32[2,2]{1,0:T(2,128)S(1)}, s32[2,2]{1,0:T(2,128)}, u32[]{:S(2)}) copy-start(s32[2,2]{1,0:T(2,128)} %owner_ref.1) | copy-start | bytes 52

commit v2 on v1

--- a/solution.py
+++ b/solution.py
@@ -94,9 +94,9 @@
     return out
 
 
-def kernel(nx, ny, pdf_ref, grains_ref, moves_ref, owner_ref, links_ref,
+def kernel(nx, ny, pdf_hbm, grains_hbm, moves_hbm, owner_hbm, links_hbm,
            blocks_ref, table_ref,
-           star, zstar, final, pad, tab, outbox, inbox, parcel,
+           pdf_ref, grains_ref, moves_ref, owner_ref, links_ref, load_sem, star, zstar, final, pad, tab, outbox, inbox, parcel,
            note_send, note_recv, block_send, block_recv, local_sem):
     gx = lax.axis_index("gx")
     gy = lax.axis_index("gy")
@@ -104,6 +104,14 @@
     def device(dx, dy):
         return (lax.rem(gx + dx + nx, nx), lax.rem(gy + dy + ny, ny))
 
+    loads = [
+        pltpu.make_async_copy(source, held, load_sem.at[i])
+        for i, (source, held) in enumerate((
+            (grains_hbm, grains_ref), (moves_hbm, moves_ref), (pdf_hbm, pdf_ref),
+            (owner_hbm, owner_ref), (links_hbm, links_ref)))
+    ]
+    for load in loads:
+        load.start()
     barrier = pltpu.get_barrier_semaphore()
     peers = [steps_of(m) for m in codes] + [(d, 0) for d in range(2, nx - 1)]
     for dx, dy in peers:
@@ -114,6 +122,8 @@
     depth = lane % 8
 
     pad[...] = jnp.zeros_like(pad)
+    for load in loads:
+        load.wait()
     own = grains_ref[:, 0, :]
     pad[0:26, :] = own
     code = moves_ref[...]
@@ -197,22 +207,39 @@
     place = half * 64 + cells % 64
     fdirs = dirs.astype(F32)
 
+    features = jnp.concatenate(list(split3(tab[0:16, 0:256])), axis=0)
+    resting, arriving, targets = [], [], []
+    for b in range(2):
+        slot = slots[b:b + 1, :]
+        chosen = jnp.where(
+            lax.broadcasted_iota(jnp.int32, (256, 512), 0) == slot, 1.0, 0.0).astype(BF16)
+        resting.append(jnp.dot(features, chosen, preferred_element_type=F32))
+        arriving.append(jnp.where(
+            lax.broadcasted_iota(jnp.int32, (128, 512), 0) + 256 == slot,
+            1.0, 0.0).astype(BF16))
+        targets.append(jnp.where(
+            lax.broadcasted_iota(jnp.int32, (128, 512), 0) == place[b:b + 1, :],
+            1.0, 0.0).astype(BF16))
+
+    for q in range(19):
+        sx, sy, _ = vel[q]
+        if sx or sy:
+            zstar[q] = roll(roll(zstar[q], 8 * sy, 1), sx, 0)
+
     for copy in notes:
-        copy.wait()
+        copy.wait_recv()
 
     incoming = inbox[:, 0:8, :].reshape(64, 128)
     incoming = jnp.concatenate([incoming, jnp.zeros((64, 128), F32)], axis=0).T
     tab[0:26, 256:384] = incoming[0:26, :]
     table_ref[...] = tab[0:26, 0:320]
-    features = jnp.concatenate(list(split3(tab[0:16, :])), axis=0)
+    features = jnp.concatenate(list(split3(tab[0:16, 256:384])), axis=0)
     dense = []
     for b in range(2):
         def at(value):
             return value[b:b + 1, :]
 
-        chosen = jnp.where(
-            lax.broadcasted_iota(jnp.int32, (384, 512), 0) == at(slots), 1.0, 0.0).astype(BF16)
-        g = jnp.dot(features, chosen, preferred_element_type=F32)
+        g = resting[b] + jnp.dot(features, arriving[b], preferred_element_type=F32)
         g = g[0:16] + g[16:32] + g[32:48]
         rel_x, rel_y, rel_z = at(mid_x) - g[0:1], at(mid_y) - g[1:2], at(mid_z) - g[2:3]
         wall_x = g[3:4] + g[7:8] * rel_z - g[8:9] * rel_y
@@ -224,9 +251,7 @@
         values = [p.astype(F32) for p in split3(correction)] + [at(fdirs)]
         spread = jnp.concatenate(
             [jnp.where(in_row, value, 0.0) for value in values], axis=0).astype(BF16)
-        where_to = jnp.where(
-            lax.broadcasted_iota(jnp.int32, (128, 512), 0) == at(place), 1.0, 0.0).astype(BF16)
-        dense.append(lax.dot_general(spread, where_to, (((1,), (1,)), ((), ())),
+        dense.append(lax.dot_general(spread, targets[b], (((1,), (1,)), ((), ())),
                                      preferred_element_type=F32))
     correction = jnp.concatenate([d[0:8] + d[8:16] + d[16:24] for d in dense], axis=0)
     link_dir = jnp.concatenate([d[24:32] for d in dense], axis=0)
@@ -240,7 +265,7 @@
             i = (plus_y if sy == 1 else minus_y).index(q)
             ghost = inbox[region_of[0, sy], 8:24, :]
             ghost = roll(ghost, -8 * i + (0 if sy == 1 else 120), 1)
-            value = jnp.where(edge_lane, ghost, roll(value, 8 * sy, 1))
+            value = jnp.where(edge_lane, roll(ghost, sx, 0), value)
         if sx:
             i = (plus_x if sx == 1 else minus_x).index(q)
             line = inbox[region_of[sx, 0], 8 + i:9 + i, :]
@@ -249,38 +274,41 @@
                 corner = inbox[region_of[sx, sy], 0:8, :]
                 corner = roll(corner, 8, 1) if sy == 1 else corner
                 line = jnp.where(edge_lane[0:8], corner, line)[0:1]
-            value = jnp.where(row == (0 if sx == 1 else 15), line, roll(value, sx, 0))
+            value = jnp.where(row == (0 if sx == 1 else 15), line, value)
         if q:
             value = jnp.where(link_dir == float(opp[q]), star[opp[q]] - correction, value)
         final[q * 16:(q + 1) * 16, :] = value
 
     wide = lax.broadcasted_iota(jnp.int32, (24, 128), 1) < 64
-    holds = [jnp.full((24, 128), owner_ref[n // 2, n % 2], jnp.int32) for n in range(4)]
+    holds = [jnp.broadcast_to(owner_ref[n // 2:n // 2 + 1, n % 2:n % 2 + 1], (24, 128))
+             for n in range(4)]
+    pieces = []
     for k in range(4):
-        pieces = []
         for b in range(2):
             first = final[pl.ds(b * 8 + 2 * k, 24, stride=16), :]
             second = final[pl.ds(b * 8 + 2 * k + 1, 24, stride=16), :]
             pieces.append(jnp.where(wide, first, roll(second, 64, 1)))
             pieces.append(jnp.where(wide, roll(first, 64, 1), second))
-        for o in range(nx):
+    sends = []
+    for d in list(range(1, nx)) + [0]:
+        to = lax.rem(gx + d, nx)
+        here = [hold == to for hold in holds]
+        for k in range(4):
             value = jnp.zeros((24, 128), F32)
             for n in range(4):
-                value = jnp.where(holds[n] == o, pieces[n], value)
-            parcel[o, :, k * 128:(k + 1) * 128] = value[0:19]
-
-    sends = []
-    for d in range(1, nx):
-        to = lax.rem(gx + d, nx)
-        copy = pltpu.make_async_remote_copy(
-            src_ref=parcel.at[to], dst_ref=blocks_ref.at[gx],
-            send_sem=block_send.at[d - 1], recv_sem=block_recv.at[d - 1],
-            device_id=(to, gy), device_id_type=MESH)
+                value = jnp.where(here[n], pieces[4 * k + n], value)
+            parcel[d, :, k * 128:(k + 1) * 128] = value[0:19]
+        if d:
+            copy = pltpu.make_async_remote_copy(
+                src_ref=parcel.at[d], dst_ref=blocks_ref.at[gx],
+                send_sem=block_send.at[d - 1], recv_sem=block_recv.at[d - 1],
+                device_id=(to, gy), device_id_type=MESH)
+        else:
+            copy = pltpu.make_async_copy(parcel.at[0], blocks_ref.at[gx], local_sem)
         copy.start()
         sends.append(copy)
-    here = pltpu.make_async_copy(parcel.at[gx], blocks_ref.at[gx], local_sem)
-    here.start()
-    here.wait()
+    for copy in notes:
+        copy.wait_send()
     for copy in sends:
         copy.wait()
 
@@ -292,9 +320,15 @@
         functools.partial(kernel, nx, ny),
         out_shape=(jax.ShapeDtypeStruct((nx, 19, 512), F32),
                    jax.ShapeDtypeStruct((26, 320), F32)),
-        in_specs=[vmem, vmem, vmem, pl.BlockSpec(memory_space=pltpu.SMEM), vmem],
+        in_specs=[pl.BlockSpec(memory_space=pltpu.HBM)] * 5,
         out_specs=(pl.BlockSpec(memory_space=pl.ANY), vmem),
         scratch_shapes=[
+            pltpu.VMEM(pdf.shape, F32),
+            pltpu.VMEM(grains.shape, F32),
+            pltpu.VMEM(grain_moves.shape, jnp.int32),
+            pltpu.VMEM(owner_map.shape, jnp.int32),
+            pltpu.VMEM(link_lists.shape, jnp.int32),
+            pltpu.SemaphoreType.DMA((5,)),
             pltpu.VMEM((19, 16, 128), F32),
             pltpu.VMEM((19, 16, 128), F32),
             pltpu.VMEM((384, 128), F32),

time: 22.1 us -> 21.8 us (0.986)
    pallas_call x1, Pallas kernels: 15.9 us -> 15.7 us  [body(): pl.pallas_call(functools.partial(kernel, nx, ny), out_shape=(jax.ShapeDty...]
where the time goes in v2:
time: 21.8 us; the launch traced here: 21.5 us
  Pallas kernels  15.7 us (72%)
  local copies, waits for them, and re-layouts  5.19 us (24%)
  between operations  0.65 us (3%)
    pallas_call x1, Pallas kernels, body(): pl.pallas_call(functools.partial(kernel, nx, ny), out_shape=(jax.ShapeDty...  15.7 us
    unnamed x12, local copies, waits for them, and re-layouts  5.19 us

profile of v2, /device:TPU:0, one launch (start us, length us, event | category | flops | bytes accessed | tf_op | source)
XLA Modules:
  0.0 21.5 jit_solution(11186135177771950789)
XLA Ops:
  0.6 0.0 copy-start
  0.6 0.9 %copy-done = f32[19,16,128]{2,1,0:T(8,128)S(1)} copy-done((f32[19,16,128]{2,1,0:T(8,128)S(1)}, f32[19,16,128]{2,1,0:T(8,128)}, u32[]{:S(2)}) %copy-start) | copy-done | bytes 155672
  1.5 0.0 copy-start.1
  1.5 0.7 %copy-done.1 = f32[26,1,256]{2,1,0:T(1,128)S(1)} copy-done((f32[26,1,256]{2,1,0:T(1,128)S(1)}, f32[26,1,256]{2,1,0:T(1,128)}, u32[]{:S(2)}) %copy-start.1) | copy-done | bytes 26648
  2.3 0.0 copy-start.2
  2.3 0.7 %copy-done.2 = s32[3,2,512]{2,1,0:T(2,128)S(1)} copy-done((s32[3,2,512]{2,1,0:T(2,128)S(1)}, s32[3,2,512]{2,1,0:T(2,128)}, u32[]{:S(2)}) %copy-start.2) | copy-done | bytes 12312
  3.0 0.0 copy-start.3
  3.0 0.7 %copy-done.3 = s32[1,256]{1,0:T(1,128)S(1)} copy-done((s32[1,256]{1,0:T(1,128)S(1)}, s32[1,256]{1,0:T(1,128)}, u32[]{:S(2)}) %copy-start.3) | copy-done | bytes 1048
  3.7 0.0 copy-start.4
  3.7 0.7 %copy-done.4 = s32[2,2]{1,0:T(2,128)S(1)} copy-done((s32[2,2]{1,0:T(2,128)S(1)}, s32[2,2]{1,0:T(2,128)}, u32[]{:S(2)}) %copy-start.4) | copy-done | bytes 40
  4.4 15.7 %slab_step.1 = (f32[4,19,512]{2,1,0:T(8,128)S(1)}, f32[26,320]{1,0:T(8,128)S(1)}) custom-call(f32[19,16,128]{2,1,0:T(8,128)S(1)} %copy-done, f32[26,1,256]{2,1,0:T(1,128)S(1)} %copy-done.1, s32[1,256]{1,0:T(1,128)S(1)} %copy-done.3, s32[2,2]{1,0:T(2,128)S(1)} %copy-done.4, s32[3,2,512]{2,1,0:T(2,128)S(1)} %copy-done.2), custom_call_target="tpu_custom_call" | custom-call | tf_op jit(solution)/shard_map/slab_step/pallas_call | solution.py:319
  20.0 0.8 %copy.7 = f32[4,1,19,512]{3,1,2,0:T(1,128)} copy(f32[4,1,19,512]{3,2,0,1:T(8,128)S(1)} %bitcast.2) | data formatting | bytes 311296
  20.8 0.7 %copy.8 = f32[26,1,320]{2,1,0:T(1,128)} copy(f32[26,1,320]{2,0,1:T(8,128)S(1)} %bitcast.3) | data formatting | bytes 66560
Async XLA Ops:
  0.6 0.9 %copy-start = (f32[19,16,128]{2,1,0:T(8,128)S(1)}, f32[19,16,128]{2,1,0:T(8,128)}, u32[]{:S(2)}) copy-start(f32[19,16,128]{2,1,0:T(8,128)} %pdf_hbm.1) | copy-start | bytes 466948
  1.5 0.7 %copy-start.1 = (f32[26,1,256]{2,1,0:T(1,128)S(1)}, f32[26,1,256]{2,1,0:T(1,128)}, u32[]{:S(2)}) copy-start(f32[26,1,256]{2,1,0:T(1,128)} %grains_hbm.1) | copy-start | bytes 79876
  2.3 0.7 %copy-start.2 = (s32[3,2,512]{2,1,0:T(2,128)S(1)}, s32[3,2,512]{2,1,0:T(2,128)}, u32[]{:S(2)}) copy-start(s32[3,2,512]{2,1,0:T(2,128)} %links_hbm.1) | copy-start | bytes 36868
  3.0 0.7 %copy-start.3 = (s32[1,256]{1,0:T(1,128)S(1)}, s32[1,256]{1,0:T(1,128)}, u32[]{:S(2)}) copy-start(s32[1,256]{1,0:T(1,128)} %moves_hbm.1) | copy-start | bytes 3076
  3.7 0.7 %copy-start.4 = (s32[2,2]{1,0:T(2,128)S(1)}, s32[2,2]{1,0:T(2,128)}, u32[]{:S(2)}) copy-start(s32[2,2]{1,0:T(2,128)} %owner_hbm.1) | copy-start | bytes 52

commit v3 on v2

--- a/solution.py
+++ b/solution.py
@@ -232,7 +232,7 @@
     incoming = inbox[:, 0:8, :].reshape(64, 128)
     incoming = jnp.concatenate([incoming, jnp.zeros((64, 128), F32)], axis=0).T
     tab[0:26, 256:384] = incoming[0:26, :]
-    table_ref[...] = tab[0:26, 0:320]
+    table_ref[:, 0, :] = tab[0:26, 0:320]
     features = jnp.concatenate(list(split3(tab[0:16, 256:384])), axis=0)
     dense = []
     for b in range(2):
@@ -297,7 +297,7 @@
             value = jnp.zeros((24, 128), F32)
             for n in range(4):
                 value = jnp.where(here[n], pieces[4 * k + n], value)
-            parcel[d, :, k * 128:(k + 1) * 128] = value[0:19]
+            parcel[d, :, 0, k * 128:(k + 1) * 128] = value[0:19]
         if d:
             copy = pltpu.make_async_remote_copy(
                 src_ref=parcel.at[d], dst_ref=blocks_ref.at[gx],
@@ -318,8 +318,8 @@
     vmem = pl.BlockSpec(memory_space=pltpu.VMEM)
     blocks, table = pl.pallas_call(
         functools.partial(kernel, nx, ny),
-        out_shape=(jax.ShapeDtypeStruct((nx, 19, 512), F32),
-                   jax.ShapeDtypeStruct((26, 320), F32)),
+        out_shape=(jax.ShapeDtypeStruct((nx, 19, 1, 512), F32),
+                   jax.ShapeDtypeStruct((26, 1, 320), F32)),
         in_specs=[pl.BlockSpec(memory_space=pltpu.HBM)] * 5,
         out_specs=(pl.BlockSpec(memory_space=pl.ANY), vmem),
         scratch_shapes=[
@@ -336,7 +336,7 @@
             pltpu.VMEM((32, 384), F32),
             pltpu.VMEM((8, 24, 128), F32),
             pltpu.VMEM((8, 24, 128), F32),
-            pltpu.VMEM((nx, 19, 512), F32),
+            pltpu.VMEM((nx, 19, 1, 512), F32),
             pltpu.SemaphoreType.DMA((8,)),
             pltpu.SemaphoreType.DMA((8,)),
             pltpu.SemaphoreType.DMA((nx - 1,)),
@@ -344,10 +344,10 @@
             pltpu.SemaphoreType.DMA,
         ],
         compiler_params=pltpu.CompilerParams(
-            collective_id=0, has_side_effects=True, vmem_limit_bytes=32 * 1024 * 1024),
+            collective_id=0, has_side_effects=True, vmem_limit_bytes=64 * 1024 * 1024 - 128 * 1024),
         name="slab_step",
     )(pdf, grains, grain_moves, owner_map, link_lists)
-    return blocks[:, None], table[:, None, :]
+    return blocks.transpose(0, 2, 1, 3), table
 
 
 def solution(mesh):

time: 21.8 us -> 19 us (0.87)
  local copies, waits for them, and re-layouts: 5.19 us -> 2.22 us
  Pallas kernels: 15.7 us -> 16 us
    unnamed x12 -> x4, local copies, waits for them, and re-layouts: 5.19 us -> 2.22 us
    pallas_call x1, Pallas kernels: 15.7 us -> 16 us  [body(): pl.pallas_call(functools.partial(kernel, nx, ny), out_shape=(jax.ShapeDty...]
where the time goes in v3:
time: 19 us; the launch traced here: 18.9 us
  Pallas kernels  16 us (84%)
  local copies, waits for them, and re-layouts  2.22 us (12%)
  between operations  0.65 us (3%)
    pallas_call x1, Pallas kernels, body(): pl.pallas_call(functools.partial(kernel, nx, ny), out_shape=(jax.ShapeDty...  16 us
    unnamed x4, local copies, waits for them, and re-layouts  2.22 us

profile of v3, /device:TPU:0, one launch (start us, length us, event | category | flops | bytes accessed | tf_op | source)
XLA Modules:
  0.0 18.9 jit_solution(10839069891038798637)
XLA Ops:
  0.6 16.0 %slab_step.1 = (f32[4,19,1,512]{3,2,1,0:T(1,128)}, f32[26,1,320]{2,1,0:T(1,128)}) custom-call(f32[19,16,128]{2,1,0:T(8,128)} %pdf_hbm.1, f32[26,1,256]{2,1,0:T(1,128)} %grains_hbm.1, s32[1,256]{1,0:T(1,128)} %moves_hbm.1, s32[2,2]{1,0:T(2,128)} %owner_hbm.1, s32[3,2,512]{2,1,0:T(2,128)} %links_hbm.1), custom_call_target="tpu_custom_call" | custom-call | tf_op jit(solution)/shard_map/slab_step/pallas_call | solution.py:319
  16.6 0.0 copy-start
  16.6 1.6 %copy.9 = f32[4,1,19,512]{3,1,2,0:T(1,128)} copy(f32[4,1,19,512]{3,1,2,0:T(1,128)} %bitcast.1) | data formatting | bytes 311296
  18.2 0.0 copy-done
  18.2 0.6 %copy.10 = f32[26,1,320]{2,1,0:T(1,128)} copy(f32[26,1,320]{2,1,0:T(1,128)S(1)} %copy-done) | data formatting | bytes 66560
Async XLA Ops:
  16.6 1.6 %copy-start = (f32[26,1,320]{2,1,0:T(1,128)S(1)}, f32[26,1,320]{2,1,0:T(1,128)}, u32[]{:S(2)}) copy-start(f32[26,1,320]{2,1,0:T(1,128)} %get-tuple-element.9) | copy-start | bytes 99844

commit v4 on v3

--- a/solution.py
+++ b/solution.py
@@ -122,7 +122,7 @@
     depth = lane % 8
 
     pad[...] = jnp.zeros_like(pad)
-    for load in loads:
+    for load in loads[:2]:
         load.wait()
     own = grains_ref[:, 0, :]
     pad[0:26, :] = own
@@ -144,6 +144,7 @@
     packed = packed + roll(packed, -32, 1) + roll(packed, -64, 1)
     packed = jnp.where(lax.broadcasted_iota(jnp.int32, (64, 128), 1) < 32, packed, 0.0)
 
+    loads[2].wait()
     collided = collide(lambda q: pdf_ref[q])
     for q in range(19):
         star[q] = collided[q]
@@ -187,6 +188,8 @@
     kept = own * jnp.where(code == 4, 1.0, 0.0)
     tab[...] = jnp.zeros_like(tab)
     tab[0:26, 0:256] = kept
+    for load in loads[3:]:
+        load.wait()
     cells, dirs, slots = links_ref[0], links_ref[1], links_ref[2]
 
     def step_along(axis):
@@ -290,7 +293,8 @@
             pieces.append(jnp.where(wide, first, roll(second, 64, 1)))
             pieces.append(jnp.where(wide, roll(first, 64, 1), second))
     sends = []
-    for d in list(range(1, nx)) + [0]:
+    order = sorted(range(1, nx), key=lambda d: abs(2 * d - nx))
+    for d in order + [0]:
         to = lax.rem(gx + d, nx)
         here = [hold == to for hold in holds]
         for k in range(4):
@@ -310,6 +314,15 @@
     for copy in notes:
         copy.wait_send()
     for copy in sends:
+        copy.wait()
+
+
+def hand_over(blocks_in, table_in, blocks_out, table_out, sem):
+    copies = [pltpu.make_async_copy(blocks_in, blocks_out, sem.at[0]),
+              pltpu.make_async_copy(table_in, table_out, sem.at[1])]
+    for copy in copies:
+        copy.start()
+    for copy in copies:
         copy.wait()
 
 
@@ -344,9 +357,19 @@
             pltpu.SemaphoreType.DMA,
         ],
         compiler_params=pltpu.CompilerParams(
-            collective_id=0, has_side_effects=True, vmem_limit_bytes=64 * 1024 * 1024 - 128 * 1024),
+            collective_id=0, has_side_effects=True, vmem_limit_bytes=64 * 1024 * 1024),
         name="slab_step",
     )(pdf, grains, grain_moves, owner_map, link_lists)
+    hbm = pl.BlockSpec(memory_space=pltpu.HBM)
+    blocks, table = pl.pallas_call(
+        hand_over,
+        out_shape=(jax.ShapeDtypeStruct(blocks.shape, F32),
+                   jax.ShapeDtypeStruct(table.shape, F32)),
+        in_specs=[hbm, hbm], out_specs=(hbm, hbm),
+        scratch_shapes=[pltpu.SemaphoreType.DMA((2,))],
+        compiler_params=pltpu.CompilerParams(vmem_limit_bytes=64 * 1024 * 1024),
+        name="hand_over",
+    )(blocks, table)
     return blocks.transpose(0, 2, 1, 3), table
 
 

time: 19 us -> 24.5 us (1.29)
  Pallas kernels: 16 us -> 23.8 us
  local copies, waits for them, and re-layouts: 2.22 us -> 0 us
    pallas_call x0 -> x1, Pallas kernels: none -> 7.05 us  [body(): pl.pallas_call(hand_over, out_shape=(jax.ShapeDtypeStruct(blocks.shape, F...]
    unnamed x4 -> x0, local copies, waits for them, and re-layouts: 2.22 us -> none
    pallas_call x1, Pallas kernels: 16 us -> 16.7 us  [body(): pl.pallas_call(functools.partial(kernel, nx, ny), out_shape=(jax.ShapeDty...]
where the time goes in v4:
time: 24.5 us; the launch traced here: 24.4 us
  Pallas kernels  23.8 us (97%)
  between operations  0.64 us (3%)
    pallas_call x1, Pallas kernels, body(): pl.pallas_call(functools.partial(kernel, nx, ny), out_shape=(jax.ShapeDty...  16.7 us
    pallas_call x1, Pallas kernels, body(): pl.pallas_call(hand_over, out_shape=(jax.ShapeDtypeStruct(blocks.shape, F...  7.05 us

profile of v4, /device:TPU:0, one launch (start us, length us, event | category | flops | bytes accessed | tf_op | source)
XLA Modules:
  0.0 24.4 jit_solution(9289979189914140178)
XLA Ops:
  0.6 16.7 %slab_step.1 = (f32[4,19,1,512]{3,2,1,0:T(1,128)}, f32[26,1,320]{2,1,0:T(1,128)}) custom-call(f32[19,16,128]{2,1,0:T(8,128)} %pdf_hbm.1, f32[26,1,256]{2,1,0:T(1,128)} %grains_hbm.1, s32[1,256]{1,0:T(1,128)} %moves_hbm.1, s32[2,2]{1,0:T(2,128)} %owner_hbm.1, s32[3,2,512]{2,1,0:T(2,128)} %links_hbm.1), custom_call_target="tpu_custom_call" | custom-call | tf_op jit(solution)/shard_map/slab_step/pallas_call | solution.py:332
  17.4 7.0 %hand_over.1 = (f32[4,19,1,512]{3,2,1,0:T(1,128)}, f32[26,1,320]{2,1,0:T(1,128)}) custom-call(f32[4,19,1,512]{3,2,1,0:T(1,128)} %get-tuple-element.6.blocks_in, f32[26,1,320]{2,1,0:T(1,128)} %get-tuple-element.7.table_in), custom_call_target="tpu_custom_call" | custom-call | tf_op jit(solution)/shard_map/hand_over/pallas_call | solution.py:364

commit v5 on v4

--- a/solution.py
+++ b/solution.py
@@ -317,13 +317,20 @@
         copy.wait()
 
 
-def hand_over(blocks_in, table_in, blocks_out, table_out, sem):
-    copies = [pltpu.make_async_copy(blocks_in, blocks_out, sem.at[0]),
-              pltpu.make_async_copy(table_in, table_out, sem.at[1])]
-    for copy in copies:
-        copy.start()
-    for copy in copies:
-        copy.wait()
+def hand_over(blocks_in, table_in, blocks_out, table_out, blocks_here, table_here,
+              load_sem, store_sem):
+    count = blocks_in.shape[0]
+    pairs = [(blocks_in.at[i], blocks_here.at[i], blocks_out.at[i]) for i in range(count)]
+    pairs.append((table_in, table_here, table_out))
+    loads = [pltpu.make_async_copy(a, b, load_sem.at[i]) for i, (a, b, _) in enumerate(pairs)]
+    stores = [pltpu.make_async_copy(b, c, store_sem.at[i]) for i, (_, b, c) in enumerate(pairs)]
+    for load in loads:
+        load.start()
+    for load, store in zip(loads, stores):
+        load.wait()
+        store.start()
+    for store in stores:
+        store.wait()
 
 
 def body(pdf, grains, grain_moves, owner_map, link_lists):
@@ -366,7 +373,12 @@
         out_shape=(jax.ShapeDtypeStruct(blocks.shape, F32),
                    jax.ShapeDtypeStruct(table.shape, F32)),
         in_specs=[hbm, hbm], out_specs=(hbm, hbm),
-        scratch_shapes=[pltpu.SemaphoreType.DMA((2,))],
+        scratch_shapes=[
+            pltpu.VMEM(blocks.shape, F32),
+            pltpu.VMEM(table.shape, F32),
+            pltpu.SemaphoreType.DMA((nx + 1,)),
+            pltpu.SemaphoreType.DMA((nx + 1,)),
+        ],
         compiler_params=pltpu.CompilerParams(vmem_limit_bytes=64 * 1024 * 1024),
         name="hand_over",
     )(blocks, table)

time: 24.5 us -> 19.1 us (0.78)
  Pallas kernels: 23.8 us -> 18.3 us
    pallas_call x1, Pallas kernels: 7.05 us -> 1.56 us  [body(): pl.pallas_call(hand_over, out_shape=(jax.ShapeDtypeStruct(blocks.shape, F...]
where the time goes in v5:
time: 19.1 us; the launch traced here: 18.9 us
  Pallas kernels  18.3 us (96%)
  between operations  0.64 us (3%)
    pallas_call x1, Pallas kernels, body(): pl.pallas_call(functools.partial(kernel, nx, ny), out_shape=(jax.ShapeDty...  16.7 us
    pallas_call x1, Pallas kernels, body(): pl.pallas_call(hand_over, out_shape=(jax.ShapeDtypeStruct(blocks.shape, F...  1.56 us

profile of v5, /device:TPU:0, one launch (start us, length us, event | category | flops | bytes accessed | tf_op | source)
XLA Modules:
  0.0 18.9 jit_solution(7413526696183313893)
XLA Ops:
  0.6 16.7 %slab_step.1 = (f32[4,19,1,512]{3,2,1,0:T(1,128)}, f32[26,1,320]{2,1,0:T(1,128)}) custom-call(f32[19,16,128]{2,1,0:T(8,128)} %pdf_hbm.1, f32[26,1,256]{2,1,0:T(1,128)} %grains_hbm.1, s32[1,256]{1,0:T(1,128)} %moves_hbm.1, s32[2,2]{1,0:T(2,128)} %owner_hbm.1, s32[3,2,512]{2,1,0:T(2,128)} %links_hbm.1), custom_call_target="tpu_custom_call" | custom-call | tf_op jit(solution)/shard_map/slab_step/pallas_call | solution.py:339
  17.4 1.6 %hand_over.1 = (f32[4,19,1,512]{3,2,1,0:T(1,128)}, f32[26,1,320]{2,1,0:T(1,128)}) custom-call(f32[4,19,1,512]{3,2,1,0:T(1,128)} %get-tuple-element.6.blocks_in, f32[26,1,320]{2,1,0:T(1,128)} %get-tuple-element.7.table_in), custom_call_target="tpu_custom_call" | custom-call | tf_op jit(solution)/shard_map/hand_over/pallas_call | solution.py:371

commit v6 on v3

--- a/solution.py
+++ b/solution.py
@@ -95,9 +95,9 @@
 
 
 def kernel(nx, ny, pdf_hbm, grains_hbm, moves_hbm, owner_hbm, links_hbm,
-           blocks_ref, table_ref,
-           pdf_ref, grains_ref, moves_ref, owner_ref, links_ref, load_sem, star, zstar, final, pad, tab, outbox, inbox, parcel,
-           note_send, note_recv, block_send, block_recv, local_sem):
+           bulk_ref, fix_ref, table_ref,
+           pdf_ref, grains_ref, moves_ref, owner_ref, links_ref, load_sem, star, zstar, pad, tab, outbox, inbox, parcel, patch,
+           note_send, note_recv, block_send, block_recv, patch_send, patch_recv, local_sem):
     gx = lax.axis_index("gx")
     gy = lax.axis_index("gy")
 
@@ -122,7 +122,7 @@
     depth = lane % 8
 
     pad[...] = jnp.zeros_like(pad)
-    for load in loads:
+    for load in loads[:2]:
         load.wait()
     own = grains_ref[:, 0, :]
     pad[0:26, :] = own
@@ -144,6 +144,7 @@
     packed = packed + roll(packed, -32, 1) + roll(packed, -64, 1)
     packed = jnp.where(lax.broadcasted_iota(jnp.int32, (64, 128), 1) < 32, packed, 0.0)
 
+    loads[2].wait()
     collided = collide(lambda q: pdf_ref[q])
     for q in range(19):
         star[q] = collided[q]
@@ -184,9 +185,48 @@
         copy.start()
         notes.append(copy)
 
+    for q in range(19):
+        sx, sy, _ = vel[q]
+        if sx or sy:
+            zstar[q] = roll(roll(zstar[q], 8 * sy, 1), sx, 0)
+    loads[3].wait()
+    holds = [jnp.broadcast_to(owner_ref[n // 2:n // 2 + 1, n % 2:n % 2 + 1], (8, 128))
+             for n in range(4)]
+    wide = lane < 64
+    sends = []
+
+    def by_block(low, high):
+        left = jnp.where(wide, low, roll(high, 64, 1))
+        right = jnp.where(wide, roll(low, 64, 1), high)
+        return [left[0:8], right[0:8], left[8:16], right[8:16]]
+
+    def to_owners(tiles, box, out_ref, send_sems, recv_sems, local):
+        for d in list(range(1, nx)) + [0]:
+            to = lax.rem(gx + d, nx)
+            mine = [hold == to for hold in holds]
+            for p, tile in enumerate(tiles):
+                value = jnp.zeros((8, 128), F32)
+                for n in range(4):
+                    value = jnp.where(mine[n], tile[n], value)
+                box[d, p] = value
+            if d:
+                copy = pltpu.make_async_remote_copy(
+                    src_ref=box.at[d], dst_ref=out_ref.at[gx],
+                    send_sem=send_sems.at[d - 1], recv_sem=recv_sems.at[d - 1],
+                    device_id=(to, gy), device_id_type=MESH)
+            else:
+                copy = pltpu.make_async_copy(box.at[0], out_ref.at[gx], local)
+            copy.start()
+            sends.append(copy)
+
+    empty = jnp.zeros((16, 128), F32)
+    to_owners([by_block(zstar[p], zstar[10 + p] if p < 9 else empty) for p in range(10)],
+              parcel, bulk_ref, block_send, block_recv, local_sem.at[0])
+
     kept = own * jnp.where(code == 4, 1.0, 0.0)
     tab[...] = jnp.zeros_like(tab)
     tab[0:26, 0:256] = kept
+    loads[4].wait()
     cells, dirs, slots = links_ref[0], links_ref[1], links_ref[2]
 
     def step_along(axis):
@@ -220,11 +260,6 @@
         targets.append(jnp.where(
             lax.broadcasted_iota(jnp.int32, (128, 512), 0) == place[b:b + 1, :],
             1.0, 0.0).astype(BF16))
-
-    for q in range(19):
-        sx, sy, _ = vel[q]
-        if sx or sy:
-            zstar[q] = roll(roll(zstar[q], 8 * sy, 1), sx, 0)
 
     for copy in notes:
         copy.wait_recv()
@@ -257,71 +292,96 @@
     link_dir = jnp.concatenate([d[24:32] for d in dense], axis=0)
 
     region_of = {steps_of(m): k for k, m in enumerate(codes)}
-    for q in range(19):
-        sx, sy, _ = vel[q]
-        value = zstar[q]
-        edge_lane = lane < 8 if sy == 1 else lane >= 120
-        if sy:
-            i = (plus_y if sy == 1 else minus_y).index(q)
-            ghost = inbox[region_of[0, sy], 8:24, :]
-            ghost = roll(ghost, -8 * i + (0 if sy == 1 else 120), 1)
-            value = jnp.where(edge_lane, roll(ghost, sx, 0), value)
-        if sx:
-            i = (plus_x if sx == 1 else minus_x).index(q)
-            line = inbox[region_of[sx, 0], 8 + i:9 + i, :]
+    value = empty
+    for q in range(1, 19):
+        value = jnp.where(link_dir == float(q), star[q], value)
+    links = by_block(value - correction, link_dir)
+    sides = {}
+    for sy, qs in ((1, plus_y), (-1, minus_y)):
+        face = inbox[region_of[0, sy], 8:24, :]
+        side = face
+        for i, q in enumerate(qs):
+            if vel[q][0]:
+                side = jnp.where(lane // 8 == i, roll(face, vel[q][0], 0), side)
+        sides[sy] = roll(side, 64, 1)
+    margins = []
+    row8, lane8 = row[0:8], lane[0:8]
+    for n in range(4):
+        sx = 1 if n < 2 else -1
+        lines = jnp.zeros((8, 128), F32)
+        for i, q in enumerate(plus_x if sx == 1 else minus_x):
+            sy = vel[q][1]
+            line = jnp.broadcast_to(inbox[region_of[sx, 0], 8 + i:9 + i, :], (8, 128))
             if sy:
-                line = roll(jnp.broadcast_to(line, (8, 128)), 8 * sy, 1)
-                corner = inbox[region_of[sx, sy], 0:8, :]
-                corner = roll(corner, 8, 1) if sy == 1 else corner
-                line = jnp.where(edge_lane[0:8], corner, line)[0:1]
-            value = jnp.where(row == (0 if sx == 1 else 15), line, value)
-        if q:
-            value = jnp.where(link_dir == float(opp[q]), star[opp[q]] - correction, value)
-        final[q * 16:(q + 1) * 16, :] = value
-
-    wide = lax.broadcasted_iota(jnp.int32, (24, 128), 1) < 64
-    holds = [jnp.broadcast_to(owner_ref[n // 2:n // 2 + 1, n % 2:n % 2 + 1], (24, 128))
-             for n in range(4)]
-    pieces = []
-    for k in range(4):
-        for b in range(2):
-            first = final[pl.ds(b * 8 + 2 * k, 24, stride=16), :]
-            second = final[pl.ds(b * 8 + 2 * k + 1, 24, stride=16), :]
-            pieces.append(jnp.where(wide, first, roll(second, 64, 1)))
-            pieces.append(jnp.where(wide, roll(first, 64, 1), second))
-    sends = []
-    for d in list(range(1, nx)) + [0]:
-        to = lax.rem(gx + d, nx)
-        here = [hold == to for hold in holds]
-        for k in range(4):
-            value = jnp.zeros((24, 128), F32)
-            for n in range(4):
-                value = jnp.where(here[n], pieces[4 * k + n], value)
-            parcel[d, :, 0, k * 128:(k + 1) * 128] = value[0:19]
-        if d:
-            copy = pltpu.make_async_remote_copy(
-                src_ref=parcel.at[d], dst_ref=blocks_ref.at[gx],
-                send_sem=block_send.at[d - 1], recv_sem=block_recv.at[d - 1],
-                device_id=(to, gy), device_id_type=MESH)
-        else:
-            copy = pltpu.make_async_copy(parcel.at[0], blocks_ref.at[gx], local_sem)
-        copy.start()
-        sends.append(copy)
+                corner = inbox[region_of[sx, sy], 0:1, :]
+                corner = roll(jnp.broadcast_to(corner, (8, 128)), 8 if sy == 1 else 0, 1)
+                line = jnp.where(lane8 < 8 if sy == 1 else lane8 >= 120, corner,
+                                 roll(line, 8 * sy, 1))
+            lines = jnp.where(row8 == i, line, lines)
+        side = sides[1 if n % 2 == 0 else -1][8 * (n // 2):8 * (n // 2) + 8]
+        margin = jnp.where(wide[0:8], roll(lines, 64, 1) if n % 2 else lines, side)
+        margin = jnp.where(lane8 == 112, float(n // 2), margin)
+        margins.append(jnp.where(lane8 == 113, float(n % 2), margin))
+    to_owners([links, margins], patch, fix_ref, patch_send, patch_recv, local_sem.at[1])
     for copy in notes:
         copy.wait_send()
     for copy in sends:
         copy.wait()
 
 
+def settle(bulk_ref, fix_ref, table_in, blocks_ref, table_ref):
+    table_ref[...] = table_in[...]
+    lane = lax.broadcasted_iota(jnp.int32, (8, 128), 1)
+    row = lax.broadcasted_iota(jnp.int32, (8, 128), 0)
+    wide = lane < 64
+    for a in range(bulk_ref.shape[0]):
+        links, margin = fix_ref[a, 0], fix_ref[a, 1]
+        turned = roll(links, 64, 1)
+        link_value = jnp.where(wide, links, turned)
+        link_dir = jnp.where(wide, turned, links)
+        at_x = jnp.broadcast_to(margin[0:1, 112:113], (8, 128))
+        at_y = jnp.broadcast_to(margin[0:1, 113:114], (8, 128))
+        for p in range(10):
+            value = bulk_ref[a, p]
+            for half, q in ((0, p), (1, 10 + p)):
+                if q > 18:
+                    continue
+                sx, sy, _ = vel[q]
+                if sy:
+                    i = (plus_y if sy == 1 else minus_y).index(q)
+                    first = 64 * half + (0 if sy == 1 else 56)
+                    inside = (lane >= first) & (lane < first + 8)
+                    inside = inside & (at_y == (0.0 if sy == 1 else 1.0))
+                    value = jnp.where(inside, roll(margin, first - 64 - 8 * i, 1), value)
+                if sx:
+                    i = (plus_x if sx == 1 else minus_x).index(q)
+                    line = jnp.broadcast_to(margin[i:i + 1, :], (8, 128))
+                    line = roll(line, 64, 1) if half else line
+                    inside = (row == (0 if sx == 1 else 7)) & (wide if half == 0 else lane >= 64)
+                    inside = inside & (at_x == (0.0 if sx == 1 else 1.0))
+                    value = jnp.where(inside, line, value)
+            wanted = jnp.where(wide, float(opp[p]) if p else -1.0,
+                               float(opp[10 + p]) if p < 9 else -1.0)
+            value = jnp.where(link_dir == wanted, link_value, value)
+            moved = roll(value, 64, 1)
+            low = jnp.where(wide, value, roll(moved, -1, 0))
+            high = jnp.where(wide, moved, roll(value, -1, 0))
+            for q, pairs in ((p, low), (10 + p, high)):
+                if q < 19:
+                    for k in range(4):
+                        blocks_ref[a, q, :, k * 128:(k + 1) * 128] = pairs[2 * k:2 * k + 1, :]
+
+
 def body(pdf, grains, grain_moves, owner_map, link_lists):
     nx, ny = lax.axis_size("gx"), lax.axis_size("gy")
     vmem = pl.BlockSpec(memory_space=pltpu.VMEM)
-    blocks, table = pl.pallas_call(
+    bulk, fix, table = pl.pallas_call(
         functools.partial(kernel, nx, ny),
-        out_shape=(jax.ShapeDtypeStruct((nx, 19, 1, 512), F32),
+        out_shape=(jax.ShapeDtypeStruct((nx, 10, 8, 128), F32),
+                   jax.ShapeDtypeStruct((nx, 2, 8, 128), F32),
                    jax.ShapeDtypeStruct((26, 1, 320), F32)),
         in_specs=[pl.BlockSpec(memory_space=pltpu.HBM)] * 5,
-        out_specs=(pl.BlockSpec(memory_space=pl.ANY), vmem),
+        out_specs=(pl.BlockSpec(memory_space=pl.ANY), pl.BlockSpec(memory_space=pl.ANY), vmem),
         scratch_shapes=[
             pltpu.VMEM(pdf.shape, F32),
             pltpu.VMEM(grains.shape, F32),
@@ -331,22 +391,32 @@
             pltpu.SemaphoreType.DMA((5,)),
             pltpu.VMEM((19, 16, 128), F32),
             pltpu.VMEM((19, 16, 128), F32),
-            pltpu.VMEM((384, 128), F32),
             pltpu.VMEM((32, 256), F32),
             pltpu.VMEM((32, 384), F32),
             pltpu.VMEM((8, 24, 128), F32),
             pltpu.VMEM((8, 24, 128), F32),
-            pltpu.VMEM((nx, 19, 1, 512), F32),
+            pltpu.VMEM((nx, 10, 8, 128), F32),
+            pltpu.VMEM((nx, 2, 8, 128), F32),
             pltpu.SemaphoreType.DMA((8,)),
             pltpu.SemaphoreType.DMA((8,)),
             pltpu.SemaphoreType.DMA((nx - 1,)),
             pltpu.SemaphoreType.DMA((nx - 1,)),
-            pltpu.SemaphoreType.DMA,
+            pltpu.SemaphoreType.DMA((nx - 1,)),
+            pltpu.SemaphoreType.DMA((nx - 1,)),
+            pltpu.SemaphoreType.DMA((2,)),
         ],
         compiler_params=pltpu.CompilerParams(
-            collective_id=0, has_side_effects=True, vmem_limit_bytes=64 * 1024 * 1024 - 128 * 1024),
+            collective_id=0, has_side_effects=True, vmem_limit_bytes=64 * 1024 * 1024),
         name="slab_step",
     )(pdf, grains, grain_moves, owner_map, link_lists)
+    blocks, table = pl.pallas_call(
+        settle,
+        out_shape=(jax.ShapeDtypeStruct((nx, 19, 1, 512), F32),
+                   jax.ShapeDtypeStruct(table.shape, F32)),
+        in_specs=[vmem] * 3, out_specs=(vmem, vmem),
+        compiler_params=pltpu.CompilerParams(vmem_limit_bytes=64 * 1024 * 1024),
+        name="settle",
+    )(bulk, fix, table)
     return blocks.transpose(0, 2, 1, 3), table
 
 

time: 19 us -> 18 us (0.947)
  local copies, waits for them, and re-layouts: 2.22 us -> 0 us
  Pallas kernels: 16 us -> 17.3 us
    unnamed x4 -> x0, local copies, waits for them, and re-layouts: 2.22 us -> none
    pallas_call x0 -> x1, Pallas kernels: none -> 1.89 us  [body(): pl.pallas_call(settle, out_shape=(jax.ShapeDtypeStruct((nx, 19, 1, 512),...]
    pallas_call x1, Pallas kernels: 16 us -> 15.4 us  [body(): pl.pallas_call(functools.partial(kernel, nx, ny), out_shape=(jax.ShapeDty...]
where the time goes in v6:
time: 18 us; the launch traced here: 17.9 us
  Pallas kernels  17.3 us (96%)
  between operations  0.64 us (4%)
    pallas_call x1, Pallas kernels, body(): pl.pallas_call(functools.partial(kernel, nx, ny), out_shape=(jax.ShapeDty...  15.4 us
    pallas_call x1, Pallas kernels, body(): pl.pallas_call(settle, out_shape=(jax.ShapeDtypeStruct((nx, 19, 1, 512),...  1.89 us

profile of v6, /device:TPU:0, one launch (start us, length us, event | category | flops | bytes accessed | tf_op | source)
XLA Modules:
  0.0 17.9 jit_solution(13685199093973037564)
XLA Ops:
  0.6 15.4 %slab_step.1 = (f32[4,10,8,128]{3,2,1,0:T(8,128)}, f32[4,2,8,128]{3,2,1,0:T(8,128)}, f32[26,1,320]{2,1,0:T(1,128)}) custom-call(f32[19,16,128]{2,1,0:T(8,128)} %pdf_hbm.1, f32[26,1,256]{2,1,0:T(1,128)} %grains_hbm.1, s32[1,256]{1,0:T(1,128)} %moves_hbm.1, s32[2,2]{1,0:T(2,128)} %owner_hbm.1, s32[3,2,512]{2,1,0:T(2,128)} %links_hbm.1), custom_call_target="tpu_custom_call" | custom-call | tf_op jit(solution)/shard_map/slab_step/pallas_call | solution.py:378
  16.0 1.9 %settle.1 = (f32[4,19,1,512]{3,2,1,0:T(1,128)}, f32[26,1,320]{2,1,0:T(1,128)}) custom-call(f32[4,10,8,128]{3,2,1,0:T(8,128)} %get-tuple-element.7.bulk_ref, f32[4,2,8,128]{3,2,1,0:T(8,128)} %get-tuple-element.8.fix_ref, f32[26,1,320]{2,1,0:T(1,128)} %get-tuple-element.9.table_in), custom_call_target="tpu_custom_call" | custom-call | tf_op jit(solution)/shard_map/settle/pallas_call | solution.py:412

commit v7 on v6

--- a/solution.py
+++ b/solution.py
@@ -377,11 +377,11 @@
     vmem = pl.BlockSpec(memory_space=pltpu.VMEM)
     bulk, fix, table = pl.pallas_call(
         functools.partial(kernel, nx, ny),
-        out_shape=(jax.ShapeDtypeStruct((nx, 10, 8, 128), F32),
-                   jax.ShapeDtypeStruct((nx, 2, 8, 128), F32),
-                   jax.ShapeDtypeStruct((26, 1, 320), F32)),
+        out_shape=(pltpu.VMEM((nx, 10, 8, 128), F32),
+                   pltpu.VMEM((nx, 2, 8, 128), F32),
+                   pltpu.VMEM((26, 1, 320), F32)),
         in_specs=[pl.BlockSpec(memory_space=pltpu.HBM)] * 5,
-        out_specs=(pl.BlockSpec(memory_space=pl.ANY), pl.BlockSpec(memory_space=pl.ANY), vmem),
+        out_specs=(vmem, vmem, vmem),
         scratch_shapes=[
             pltpu.VMEM(pdf.shape, F32),
             pltpu.VMEM(grains.shape, F32),
@@ -406,7 +406,7 @@
             pltpu.SemaphoreType.DMA((2,)),
         ],
         compiler_params=pltpu.CompilerParams(
-            collective_id=0, has_side_effects=True, vmem_limit_bytes=64 * 1024 * 1024),
+            collective_id=0, has_side_effects=True, vmem_limit_bytes=60 * 1024 * 1024),
         name="slab_step",
     )(pdf, grains, grain_moves, owner_map, link_lists)
     blocks, table = pl.pallas_call(
@@ -414,7 +414,7 @@
         out_shape=(jax.ShapeDtypeStruct((nx, 19, 1, 512), F32),
                    jax.ShapeDtypeStruct(table.shape, F32)),
         in_specs=[vmem] * 3, out_specs=(vmem, vmem),
-        compiler_params=pltpu.CompilerParams(vmem_limit_bytes=64 * 1024 * 1024),
+        compiler_params=pltpu.CompilerParams(vmem_limit_bytes=24 * 1024 * 1024),
         name="settle",
     )(bulk, fix, table)
     return blocks.transpose(0, 2, 1, 3), table

time: 18 us -> 16.4 us (0.911)
  Pallas kernels: 17.3 us -> 15.6 us
    pallas_call x1, Pallas kernels: 1.89 us -> 0.94 us  [body(): pl.pallas_call(settle, out_shape=(jax.ShapeDtypeStruct((nx, 19, 1, 512),...]
    pallas_call x1, Pallas kernels: 15.4 us -> 14.7 us  [body(): pl.pallas_call(functools.partial(kernel, nx, ny), out_shape=(pltpu.VMEM((...]
where the time goes in v7:
time: 16.4 us; the launch traced here: 16.2 us
  Pallas kernels  15.6 us (95%)
  between operations  0.64 us (4%)
    pallas_call x1, Pallas kernels, body(): pl.pallas_call(functools.partial(kernel, nx, ny), out_shape=(pltpu.VMEM((...  14.7 us
    pallas_call x1, Pallas kernels, body(): pl.pallas_call(settle, out_shape=(jax.ShapeDtypeStruct((nx, 19, 1, 512),...  0.94 us

profile of v7, /device:TPU:0, one launch (start us, length us, event | category | flops | bytes accessed | tf_op | source)
XLA Modules:
  0.0 16.2 jit_solution(14177246588157104256)
XLA Ops:
  0.6 14.7 %slab_step.1 = (f32[4,10,8,128]{3,2,1,0:T(8,128)S(1)}, f32[4,2,8,128]{3,2,1,0:T(8,128)S(1)}, f32[26,1,320]{2,1,0:T(1,128)S(1)}) custom-call(f32[19,16,128]{2,1,0:T(8,128)} %pdf_hbm.1, f32[26,1,256]{2,1,0:T(1,128)} %grains_hbm.1, s32[1,256]{1,0:T(1,128)} %moves_hbm.1, s32[2,2]{1,0:T(2,128)} %owner_hbm.1, s32[3,2,512]{2,1,0:T(2,128)} %links_hbm.1), custom_call_target="tpu_custom_call" | custom-call | tf_op jit(solution)/shard_map/slab_step/pallas_call | solution.py:378
  15.3 0.9 %settle.1 = (f32[4,19,1,512]{3,2,1,0:T(1,128)}, f32[26,1,320]{2,1,0:T(1,128)}) custom-call(f32[4,10,8,128]{3,2,1,0:T(8,128)S(1)} %get-tuple-element.7.bulk_ref, f32[4,2,8,128]{3,2,1,0:T(8,128)S(1)} %get-tuple-element.8.fix_ref, f32[26,1,320]{2,1,0:T(1,128)S(1)} %get-tuple-element.9.table_in), custom_call_target="tpu_custom_call" | custom-call | tf_op jit(solution)/shard_map/settle/pallas_call | solution.py:412

commit v8 on v7

--- a/solution.py
+++ b/solution.py
@@ -104,6 +104,11 @@
     def device(dx, dy):
         return (lax.rem(gx + dx + nx, nx), lax.rem(gy + dy + ny, ny))
 
+    barrier = pltpu.get_barrier_semaphore()
+    peers = [steps_of(m) for m in codes] + [(d, 0) for d in range(2, nx - 1)]
+    for dx, dy in peers:
+        pl.semaphore_signal(barrier, inc=1, device_id=device(dx, dy), device_id_type=MESH)
+
     loads = [
         pltpu.make_async_copy(source, held, load_sem.at[i])
         for i, (source, held) in enumerate((
@@ -112,11 +117,6 @@
     ]
     for load in loads:
         load.start()
-    barrier = pltpu.get_barrier_semaphore()
-    peers = [steps_of(m) for m in codes] + [(d, 0) for d in range(2, nx - 1)]
-    for dx, dy in peers:
-        pl.semaphore_signal(barrier, inc=1, device_id=device(dx, dy), device_id_type=MESH)
-
     lane = lax.broadcasted_iota(jnp.int32, (16, 128), 1)
     row = lax.broadcasted_iota(jnp.int32, (16, 128), 0)
     depth = lane % 8
@@ -329,8 +329,10 @@
         copy.wait()
 
 
-def settle(bulk_ref, fix_ref, table_in, blocks_ref, table_ref):
-    table_ref[...] = table_in[...]
+def settle(bulk_ref, fix_ref, table_in, blocks_out, table_out, blocks_ref, sem):
+    count = bulk_ref.shape[0]
+    stores = [pltpu.make_async_copy(table_in, table_out, sem.at[count])]
+    stores[0].start()
     lane = lax.broadcasted_iota(jnp.int32, (8, 128), 1)
     row = lax.broadcasted_iota(jnp.int32, (8, 128), 0)
     wide = lane < 64
@@ -370,6 +372,11 @@
                 if q < 19:
                     for k in range(4):
                         blocks_ref[a, q, :, k * 128:(k + 1) * 128] = pairs[2 * k:2 * k + 1, :]
+        store = pltpu.make_async_copy(blocks_ref.at[a], blocks_out.at[a], sem.at[a])
+        store.start()
+        stores.append(store)
+    for store in stores:
+        store.wait()
 
 
 def body(pdf, grains, grain_moves, owner_map, link_lists):
@@ -413,7 +420,9 @@
         settle,
         out_shape=(jax.ShapeDtypeStruct((nx, 19, 1, 512), F32),
                    jax.ShapeDtypeStruct(table.shape, F32)),
-        in_specs=[vmem] * 3, out_specs=(vmem, vmem),
+        in_specs=[vmem] * 3, out_specs=(pl.BlockSpec(memory_space=pltpu.HBM),) * 2,
+        scratch_shapes=[pltpu.VMEM((nx, 19, 1, 512), F32),
+                        pltpu.SemaphoreType.DMA((nx + 1,))],
         compiler_params=pltpu.CompilerParams(vmem_limit_bytes=24 * 1024 * 1024),
         name="settle",
     )(bulk, fix, table)

time: 16.4 us -> 16.4 us (level)
  no operation moved by 1% of the time
where the time goes in v8:
time: 16.4 us; the launch traced here: 16.3 us
  Pallas kernels  15.6 us (95%)
  between operations  0.64 us (4%)
    pallas_call x1, Pallas kernels, body(): pl.pallas_call(functools.partial(kernel, nx, ny), out_shape=(pltpu.VMEM((...  14.7 us
    pallas_call x1, Pallas kernels, body(): pl.pallas_call(settle, out_shape=(jax.ShapeDtypeStruct((nx, 19, 1, 512),...  0.98 us

profile of v8, /device:TPU:0, one launch (start us, length us, event | category | flops | bytes accessed | tf_op | source)
XLA Modules:
  0.0 16.3 jit_solution(7025139344805448450)
XLA Ops:
  0.6 14.7 %slab_step.1 = (f32[4,10,8,128]{3,2,1,0:T(8,128)S(1)}, f32[4,2,8,128]{3,2,1,0:T(8,128)S(1)}, f32[26,1,320]{2,1,0:T(1,128)S(1)}) custom-call(f32[19,16,128]{2,1,0:T(8,128)} %pdf_hbm.1, f32[26,1,256]{2,1,0:T(1,128)} %grains_hbm.1, s32[1,256]{1,0:T(1,128)} %moves_hbm.1, s32[2,2]{1,0:T(2,128)} %owner_hbm.1, s32[3,2,512]{2,1,0:T(2,128)} %links_hbm.1), custom_call_target="tpu_custom_call" | custom-call | tf_op jit(solution)/shard_map/slab_step/pallas_call | solution.py:385
  15.3 1.0 %settle.1 = (f32[4,19,1,512]{3,2,1,0:T(1,128)}, f32[26,1,320]{2,1,0:T(1,128)}) custom-call(f32[4,10,8,128]{3,2,1,0:T(8,128)S(1)} %get-tuple-element.7.bulk_ref, f32[4,2,8,128]{3,2,1,0:T(8,128)S(1)} %get-tuple-element.8.fix_ref, f32[26,1,320]{2,1,0:T(1,128)S(1)} %get-tuple-element.9.table_in), custom_call_target="tpu_custom_call" | custom-call | tf_op jit(solution)/shard_map/settle/pallas_call | solution.py:419
